TPU v7x, 32 devices: a whole 2x2x4 slice. The times are simulated.
32 devices in a mesh: group: 4 (over y, x), leaf: 8 (over z, core).
Axes of the slice: x: 2, y: 2, z: 4, core: 2. Of those that a mesh axis runs over, the one named last changes fastest.
Arguments:
- right_sides: float32 [16, 131072], P(None, ('group', 'leaf')), may hold values from -6 to 6
- near_blocks: float32 [2048, 8, 4096], P(('group', 'leaf')), may hold values from -0.375 to 0.375
- near_source: int32 [2048, 8], P(('group', 'leaf')), may hold values from 0 to 2047, as said below
- near_count: int32 [2048], P(('group', 'leaf')), may hold values from 1 to 8
- basis: float32 [2048, 2048], P(('group', 'leaf')), may hold values from -0.75 to 0.75
- leaf_source: int32 [2048, 8], P(('group', 'leaf')), may hold values from 0 to 2047
- leaf_coupling: float32 [2048, 8, 1024], P(('group', 'leaf')), may hold values from -0.375 to 0.375
- leaf_transfer: float32 [2048, 1024], P(('group', 'leaf')), may hold values from -1 to 1
- cluster_source: int32 [128, 8], P(('group', 'leaf')), may hold values from 0 to 31
- cluster_coupling: float32 [128, 8, 1024], P(('group', 'leaf')), may hold values from -0.09375 to 0.09375
- cluster_transfer: float32 [128, 1024], P(('group', 'leaf')), may hold values from -1 to 1
- group_coupling: float32 [4, 4, 1024], P('group'), may hold values from -0.0234375 to 0.0234375
Outputs:
- applied: float32 [16, 131072], P(None, ('group', 'leaf'))
Inputs may be any that keep to these rules, and one draw needn't show every extreme that they name: near_source[t, j] and leaf_source[t, j] name a leaf held by the same device as t or by the device just before or after it in the order of devices.
All inputs are finite; a program needn't handle non-finite values.
Results may differ from a plain program's by a relative error of at most 0.0001.
Values sent between devices are 32-bit elements; how exact they have to be, the bound alone decides.
A program may use at most 128 MiB of HBM per device.

v0:
```python
import jax
import jax.numpy as jnp
from jax import lax
from jax.sharding import PartitionSpec as P

LEAF = 64
K = 32
RHS = 16
FAR0 = 8
FAR1 = 8


highest_precision = lax.Precision.HIGHEST


def extended(value, sides, width):
    for axis, dim in sides:
        size, length = (lax.axis_size(axis), value.shape[dim])
        up = [(i, (i + 1) % size) for i in range(size - 1)]
        down = [(j, i) for i, j in up]
        last = lax.slice_in_dim(value, length - width, length, axis=dim)
        leading = lax.slice_in_dim(value, 0, width, axis=dim)
        before = lax.ppermute(last, axis, up)
        after = lax.ppermute(leading, axis, down)
        value = jnp.concatenate([before, value, after], axis=dim)
    return value


def per_device(
    right_sides,
    near_blocks,
    near_source,
    near_count,
    basis,
    leaf_source,
    leaf_coupling,
    leaf_transfer,
    cluster_source,
    cluster_coupling,
    cluster_transfer,
    group_coupling,
):
    leaves_here = near_blocks.shape[0]
    clusters_here = cluster_coupling.shape[0]
    ngroups = lax.axis_size("group")
    device = lax.axis_index(("group", "leaf"))
    blocks = right_sides.reshape(RHS, leaves_here, LEAF).transpose(1, 0, 2)
    bases = basis.reshape(leaves_here, K, LEAF)
    leaf_coef = jnp.einsum("tka,tra->tkr", bases, blocks, precision=highest_precision)
    coef_rows = leaf_coef.transpose(2, 0, 1).reshape(RHS, leaves_here * K)
    point_ext = extended(right_sides, ((("group", "leaf"), 1),), leaves_here * LEAF)
    coef_ext = extended(coef_rows, ((("group", "leaf"), 1),), leaves_here * K)
    window_start = (device - 1) * leaves_here
    near_local = near_source - window_start
    point_blocks = point_ext.reshape(RHS, 3 * leaves_here, LEAF).transpose(1, 0, 2)
    busiest = jnp.max(near_count)

    def near_step(slot_index, running):
        picked = jnp.take(point_blocks, near_local[:, slot_index], axis=0)
        slab = lax.dynamic_index_in_dim(near_blocks, slot_index, axis=1, keepdims=False).reshape(
            leaves_here, LEAF, LEAF
        )
        live = (near_count > slot_index).astype(jnp.float32)
        term = jnp.einsum("tab,trb->tra", slab, picked, precision=highest_precision)
        return running + term * live[:, None, None]

    near_total = lax.fori_loop(
        0, busiest, near_step, jnp.zeros((leaves_here, RHS, LEAF), jnp.float32)
    )
    coef_blocks = coef_ext.reshape(RHS, 3 * leaves_here, K)
    picked_coef = jnp.take(coef_blocks, leaf_source - window_start, axis=1)
    leaf_far = jnp.einsum(
        "tjkl,rtjl->tkr",
        leaf_coupling.reshape(leaves_here, FAR0, K, K),
        picked_coef,
        precision=highest_precision,
    )
    transfers = leaf_transfer.reshape(leaves_here, K, K)
    lifted = jnp.einsum("tkl,tlr->tkr", transfers, leaf_coef, precision=highest_precision)
    cluster_coef = lifted.reshape(clusters_here, leaves_here // clusters_here, K, RHS).sum(axis=1)
    cluster_rows = cluster_coef.reshape(clusters_here, K * RHS)
    couplings = cluster_coupling.reshape(clusters_here, FAR1, K, K)
    shard_rows = lax.all_gather(cluster_rows, "leaf", axis=0, tiled=True)
    onehot = (cluster_source[:, :, None] == jnp.arange(shard_rows.shape[0])[None, None, :]).astype(
        jnp.float32
    )
    selected = jnp.einsum("ujn,nm->ujm", onehot, shard_rows, precision=highest_precision)
    selected = selected.reshape(clusters_here, FAR1, K, RHS)
    cluster_far = jnp.einsum("ujkl,ujlr->ukr", couplings, selected, precision=highest_precision)
    upper = cluster_transfer.reshape(clusters_here, K, K)
    projected = jnp.einsum("ukl,ulr->ukr", upper, cluster_coef, precision=highest_precision)
    projected_sum = projected.sum(axis=0).reshape(1, K * RHS)
    group_sum = lax.psum(projected_sum, "leaf")
    all_groups = lax.all_gather(group_sum, "group", axis=0, tiled=True)
    group_field = jnp.einsum(
        "hkl,hlr->kr",
        group_coupling.reshape(ngroups, K, K),
        all_groups.reshape(ngroups, K, RHS),
        precision=highest_precision,
    )
    cluster_field = cluster_far + jnp.einsum(
        "ulk,lr->ukr", upper, group_field, precision=highest_precision
    )
    spread_cluster = jnp.repeat(cluster_field, leaves_here // clusters_here, axis=0)
    leaf_field = leaf_far + jnp.einsum(
        "tlk,tlr->tkr", transfers, spread_cluster, precision=highest_precision
    )
    total = near_total + jnp.einsum("tka,tkr->tra", bases, leaf_field, precision=highest_precision)
    return total.transpose(1, 0, 2).reshape(RHS, leaves_here * LEAF)


def solution(mesh):
    in_specs = (
        P(None, ("group", "leaf")),
        P(("group", "leaf"), None, None),
        P(("group", "leaf"), None),
        P(("group", "leaf")),
        P(("group", "leaf"), None),
        P(("group", "leaf"), None),
        P(("group", "leaf"), None, None),
        P(("group", "leaf"), None),
        P(("group", "leaf"), None),
        P(("group", "leaf"), None, None),
        P(("group", "leaf"), None),
        P("group", None, None),
    )
    out_specs = P(None, ("group", "leaf"))
    return jax.shard_map(
        per_device, mesh=mesh, in_specs=in_specs, out_specs=out_specs, check_vma=False
    )
```

profile of v0, /device:TPU:0, one launch (start us, length us, event | category | flops | bytes accessed | tf_op | source)
XLA Modules:
  0.0 223.7 jit_solution(5856036347733792026)
XLA Ops:
  0.0 1.4 collective-permute-start.1
  1.4 3.7 %collective-permute-start = (f32[16,4096]{1,0:T(8,128)}, f32[16,4096]{1,0:T(8,128)}, u32[]{:S(2)}, u32[]{:S(2)}) collective-permute-start(f32[16,4096]{1,0:T(8,128)} %param.14), channel_id=1, source_target_pairs={{0,1},{1,2},{2,3},{3,4},{4,5},{5,6},{6,7},{7,8},{8,9},{9,10},{10,1... | collective-permute-start | bytes 786440 | tf_op jit(solution)/shard_map/ppermute | solution.py:23
  5.2 1.1 reshape.73
  6.3 1.5 reshape.72
  7.8 2.0 fusion.15
  10.9 1.3 collective-permute-start.3
  12.2 5.2 %collective-permute-start.2 = (f32[16,2048]{1,0:T(8,128)}, f32[16,2048]{1,0:T(8,128)}, u32[]{:S(2)}, u32[]{:S(2)}) collective-permute-start(f32[16,2048]{1,0:T(8,128)} %reshape.74), channel_id=1, source_target_pairs={{0,1},{1,2},{2,3},{3,4},{4,5},{5,6},{6,7},{7,8},{8,9},{9,10},{10,1... | collective-permute-start | bytes 393224 | tf_op jit(solution)/shard_map/ppermute | solution.py:23
  18.5 1.7 bitcast_reduce_fusion
  20.4 20.1 %all-gather = f32[8,4,512]{2,1,0:T(4,128)S(1)} all-gather(f32[1,4,512]{2,1,0:T(4,128)S(1)} %reshape.105), channel_id=1, replica_groups=mesh['group'=4,'leaf'=8] {'leaf'}, dimensions={0}, use_global_device_ids=true | all-gather | bytes 73728 | tf_op jit(solution)/shard_map/all_gather | solution.py:83
  43.3 14.1 %psum.7 = f32[1,512]{1,0:T(1,128)S(1)} all-reduce(f32[1,512]{1,0:T(1,128)S(1)} %reshape.82), channel_id=1, replica_groups=mesh['group'=4,'leaf'=8] {'leaf'}, use_global_device_ids=true, to_apply=%region_4.5 | all-reduce | flops 512 | bytes 4096 | tf_op jit(solution)/shard_map/psum | solution.py:93
  57.4 10.0 %all-gather.1 = f32[4,1,512]{2,1,0:T(1,128)S(1)} all-gather(f32[1,1,512]{2,1,0:T(1,128)S(1)} %bitcast.75), channel_id=1, replica_groups=mesh['group'=4,'leaf'=8] {'group'}, dimensions={0}, use_global_device_ids=true | all-gather | bytes 10240 | tf_op jit(solution)/shard_map/all_gather | solution.py:94
  67.7 2.0 convolution_bitcast_fusion.1
  70.2 3.8 %copy.82 = f32[64,8,1024]{0,2,1:T(8,128)} copy(f32[64,8,1024]{2,1,0:T(8,128)} %param.20) | data formatting | bytes 4194304 | tf_op args[6]
  74.0 9.1 %copy.83 = f32[64,8,32,32]{3,2,1,0:T(8,128)} copy(f32[64,8,32,32]{0,3,2,1:T(8,128)} %bitcast.67) | data formatting | bytes 4194304 | tf_op jit(solution)/shard_map/reshape | solution.py:74
  84.1 1.1 concatenate.13
  85.1 1.2 copy.80
  86.3 1.1 concatenate.12
  87.7 1.1 pad_maximum_fusion
  88.8 3.1 %gather_fusion.1 = f32[512,16,32]{2,1,0:T(8,128)} fusion(f32[16,192,32]{2,0,1:T(8,128)S(1)} %pad_maximum_fusion, s32[1024]{0:T(1024)S(1)} %pad_clamp_fusion.1), kind=kCustom, calls=%fused_computation.1 | custom fusion | bytes 2099200 | tf_op jit(solution)/shard_map/jit(_take)/gather | solution.py:71
  91.9 10.6 %fusion.10 = f32[64,16,32]{2,1,0:T(8,128)S(1)} fusion(f32[64,8,32,32]{3,2,1,0:T(8,128)} %copy.83, f32[64,8,16,32]{3,2,1,0:T(8,128)} %bitcast.68, pred[64,8]{1,0:T(8,128)(4,1)S(1)} %copy.76), kind=kOutput, calls=%fused_computation.19 | convolution fusion | flops 100925440 | bytes 3277312 | tf_op jit(solution)/shard_map/tjkl,rtjl->tkr/dot_general | solution.py:72
  102.5 1.8 convolution_add_fusion.1
  106.0 2.1 copy.74
  108.9 111.1 %while.10 = (s32[]{:T(128)}, f32[64,16,64]{2,1,0:T(8,128)}, s32[]{:T(128)}, s32[64,8]{0,1:T(8,128)S(1)}, f32[192,16,64]{2,1,0:T(8,128)}, /*index=5*/f32[64,8,409...) while((s32[]{:T(128)}, f32[64,16,64]{2,1,0:T(8,128)}, s32[]{:T(128)}, ...), condition=%wide.region_2.0_spmd, body=%wide.region_1.2_spmd.sunk | while | flops 50529796 | bytes 8656923 | solution.py:67
  109.7 4.4 %constant_dynamic-slice_fusion.2 = f32[64,1,4096]{2,1,0:T(1,128)S(1)} fusion(f32[64,8,4096]{2,1,0:T(8,128)} %get-tuple-element.170, s32[]{:T(128)S(6)} %select_n.43), kind=kLoop, calls=%fused_computation.11.clone.1 | loop fusion | bytes 2097156 | tf_op jit(solution)/shard_map/while/body/jit(dynamic_index_in_dim)/dynamic_slice | solution.py:60
  115.7 2.0 gather_fusion
  117.7 5.3 %fusion.45 = f32[64,16,64]{2,1,0:T(8,128)} fusion(f32[64,16,64]{2,1,0:T(8,128)} %get-tuple-element.156, f32[64,64,64]{2,1,0:T(8,128)S(1)} %reshape.124, f32[64,16,64]{2,1,0:T(8,128)S(1)} %gather_fusion, f32[64]{0:T(128)S(1)} %compare_convert_fusion.2, pred[64]{0:T(512)(128)(4,1)S(1)} %get-tuple-element.144), kind=kOutput, calls=%fused_computation.3.clone.1 | convolution fusion | flops 50528256 | bytes 1835328 | tf_op jit(solution)/shard_map/while/body/tab,trb->tra/dot_general | solution.py:64
  123.5 4.4 %constant_dynamic-slice_fusion.2 = f32[64,1,4096]{2,1,0:T(1,128)S(1)} fusion(f32[64,8,4096]{2,1,0:T(8,128)} %get-tuple-element.170, s32[]{:T(128)S(6)} %select_n.43), kind=kLoop, calls=%fused_computation.11.clone.1 | loop fusion | bytes 2097156 | tf_op jit(solution)/shard_map/while/body/jit(dynamic_index_in_dim)/dynamic_slice | solution.py:60
  129.4 2.0 gather_fusion
  131.5 5.3 %fusion.45 = f32[64,16,64]{2,1,0:T(8,128)} fusion(f32[64,16,64]{2,1,0:T(8,128)} %get-tuple-element.156, f32[64,64,64]{2,1,0:T(8,128)S(1)} %reshape.124, f32[64,16,64]{2,1,0:T(8,128)S(1)} %gather_fusion, f32[64]{0:T(128)S(1)} %compare_convert_fusion.2, pred[64]{0:T(512)(128)(4,1)S(1)} %get-tuple-element.144), kind=kOutput, calls=%fused_computation.3.clone.1 | convolution fusion | flops 50528256 | bytes 1835328 | tf_op jit(solution)/shard_map/while/body/tab,trb->tra/dot_general | solution.py:64
  137.3 4.4 %constant_dynamic-slice_fusion.2 = f32[64,1,4096]{2,1,0:T(1,128)S(1)} fusion(f32[64,8,4096]{2,1,0:T(8,128)} %get-tuple-element.170, s32[]{:T(128)S(6)} %select_n.43), kind=kLoop, calls=%fused_computation.11.clone.1 | loop fusion | bytes 2097156 | tf_op jit(solution)/shard_map/while/body/jit(dynamic_index_in_dim)/dynamic_slice | solution.py:60
  143.2 2.0 gather_fusion
  145.3 5.3 %fusion.45 = f32[64,16,64]{2,1,0:T(8,128)} fusion(f32[64,16,64]{2,1,0:T(8,128)} %get-tuple-element.156, f32[64,64,64]{2,1,0:T(8,128)S(1)} %reshape.124, f32[64,16,64]{2,1,0:T(8,128)S(1)} %gather_fusion, f32[64]{0:T(128)S(1)} %compare_convert_fusion.2, pred[64]{0:T(512)(128)(4,1)S(1)} %get-tuple-element.144), kind=kOutput, calls=%fused_computation.3.clone.1 | convolution fusion | flops 50528256 | bytes 1835328 | tf_op jit(solution)/shard_map/while/body/tab,trb->tra/dot_general | solution.py:64
  151.1 4.4 %constant_dynamic-slice_fusion.2 = f32[64,1,4096]{2,1,0:T(1,128)S(1)} fusion(f32[64,8,4096]{2,1,0:T(8,128)} %get-tuple-element.170, s32[]{:T(128)S(6)} %select_n.43), kind=kLoop, calls=%fused_computation.11.clone.1 | loop fusion | bytes 2097156 | tf_op jit(solution)/shard_map/while/body/jit(dynamic_index_in_dim)/dynamic_slice | solution.py:60
  157.0 2.0 gather_fusion
  159.0 5.3 %fusion.45 = f32[64,16,64]{2,1,0:T(8,128)} fusion(f32[64,16,64]{2,1,0:T(8,128)} %get-tuple-element.156, f32[64,64,64]{2,1,0:T(8,128)S(1)} %reshape.124, f32[64,16,64]{2,1,0:T(8,128)S(1)} %gather_fusion, f32[64]{0:T(128)S(1)} %compare_convert_fusion.2, pred[64]{0:T(512)(128)(4,1)S(1)} %get-tuple-element.144), kind=kOutput, calls=%fused_computation.3.clone.1 | convolution fusion | flops 50528256 | bytes 1835328 | tf_op jit(solution)/shard_map/while/body/tab,trb->tra/dot_general | solution.py:64
  164.9 4.4 %constant_dynamic-slice_fusion.2 = f32[64,1,4096]{2,1,0:T(1,128)S(1)} fusion(f32[64,8,4096]{2,1,0:T(8,128)} %get-tuple-element.170, s32[]{:T(128)S(6)} %select_n.43), kind=kLoop, calls=%fused_computation.11.clone.1 | loop fusion | bytes 2097156 | tf_op jit(solution)/shard_map/while/body/jit(dynamic_index_in_dim)/dynamic_slice | solution.py:60
  170.8 2.0 gather_fusion
  172.8 5.3 %fusion.45 = f32[64,16,64]{2,1,0:T(8,128)} fusion(f32[64,16,64]{2,1,0:T(8,128)} %get-tuple-element.156, f32[64,64,64]{2,1,0:T(8,128)S(1)} %reshape.124, f32[64,16,64]{2,1,0:T(8,128)S(1)} %gather_fusion, f32[64]{0:T(128)S(1)} %compare_convert_fusion.2, pred[64]{0:T(512)(128)(4,1)S(1)} %get-tuple-element.144), kind=kOutput, calls=%fused_computation.3.clone.1 | convolution fusion | flops 50528256 | bytes 1835328 | tf_op jit(solution)/shard_map/while/body/tab,trb->tra/dot_general | solution.py:64
  178.7 4.4 %constant_dynamic-slice_fusion.2 = f32[64,1,4096]{2,1,0:T(1,128)S(1)} fusion(f32[64,8,4096]{2,1,0:T(8,128)} %get-tuple-element.170, s32[]{:T(128)S(6)} %select_n.43), kind=kLoop, calls=%fused_computation.11.clone.1 | loop fusion | bytes 2097156 | tf_op jit(solution)/shard_map/while/body/jit(dynamic_index_in_dim)/dynamic_slice | solution.py:60
  184.6 2.0 gather_fusion
  186.6 5.3 %fusion.45 = f32[64,16,64]{2,1,0:T(8,128)} fusion(f32[64,16,64]{2,1,0:T(8,128)} %get-tuple-element.156, f32[64,64,64]{2,1,0:T(8,128)S(1)} %reshape.124, f32[64,16,64]{2,1,0:T(8,128)S(1)} %gather_fusion, f32[64]{0:T(128)S(1)} %compare_convert_fusion.2, pred[64]{0:T(512)(128)(4,1)S(1)} %get-tuple-element.144), kind=kOutput, calls=%fused_computation.3.clone.1 | convolution fusion | flops 50528256 | bytes 1835328 | tf_op jit(solution)/shard_map/while/body/tab,trb->tra/dot_general | solution.py:64
  192.5 4.4 %constant_dynamic-slice_fusion.2 = f32[64,1,4096]{2,1,0:T(1,128)S(1)} fusion(f32[64,8,4096]{2,1,0:T(8,128)} %get-tuple-element.170, s32[]{:T(128)S(6)} %select_n.43), kind=kLoop, calls=%fused_computation.11.clone.1 | loop fusion | bytes 2097156 | tf_op jit(solution)/shard_map/while/body/jit(dynamic_index_in_dim)/dynamic_slice | solution.py:60
  198.4 2.0 gather_fusion
  200.4 5.3 %fusion.45 = f32[64,16,64]{2,1,0:T(8,128)} fusion(f32[64,16,64]{2,1,0:T(8,128)} %get-tuple-element.156, f32[64,64,64]{2,1,0:T(8,128)S(1)} %reshape.124, f32[64,16,64]{2,1,0:T(8,128)S(1)} %gather_fusion, f32[64]{0:T(128)S(1)} %compare_convert_fusion.2, pred[64]{0:T(512)(128)(4,1)S(1)} %get-tuple-element.144), kind=kOutput, calls=%fused_computation.3.clone.1 | convolution fusion | flops 50528256 | bytes 1835328 | tf_op jit(solution)/shard_map/while/body/tab,trb->tra/dot_general | solution.py:64
  206.2 4.4 %constant_dynamic-slice_fusion.2 = f32[64,1,4096]{2,1,0:T(1,128)S(1)} fusion(f32[64,8,4096]{2,1,0:T(8,128)} %get-tuple-element.170, s32[]{:T(128)S(6)} %select_n.43), kind=kLoop, calls=%fused_computation.11.clone.1 | loop fusion | bytes 2097156 | tf_op jit(solution)/shard_map/while/body/jit(dynamic_index_in_dim)/dynamic_slice | solution.py:60
  212.2 2.0 gather_fusion
  214.2 5.3 %fusion.45 = f32[64,16,64]{2,1,0:T(8,128)} fusion(f32[64,16,64]{2,1,0:T(8,128)} %get-tuple-element.156, f32[64,64,64]{2,1,0:T(8,128)S(1)} %reshape.124, f32[64,16,64]{2,1,0:T(8,128)S(1)} %gather_fusion, f32[64]{0:T(128)S(1)} %compare_convert_fusion.2, pred[64]{0:T(512)(128)(4,1)S(1)} %get-tuple-element.144), kind=kOutput, calls=%fused_computation.3.clone.1 | convolution fusion | flops 50528256 | bytes 1835328 | tf_op jit(solution)/shard_map/while/body/tab,trb->tra/dot_general | solution.py:64
  220.0 2.6 %fusion.13 = f32[16,64,64]{2,0,1:T(8,128)S(1)} fusion(f32[64,16,64]{2,1,0:T(8,128)} %get-tuple-element.43, f32[64,16,32]{2,1,0:T(8,128)} %convolution_add_fusion.1, f32[64,32,64]{2,1,0:T(8,128)} %copy-done), kind=kOutput, calls=%fused_computation.21 | convolution fusion | flops 25231360 | bytes 1179648 | tf_op jit(solution)/shard_map/tka,tkr->tra/dot_general | solution.py:108
  (95 shorter events, 22.3 us)
Async XLA Ops:
  0.0 17.3 %copy-start.2 = (f32[64,1024]{1,0:T(8,128)S(1)}, f32[64,1024]{1,0:T(8,128)}, u32[]{:S(2)}) copy-start(f32[64,1024]{1,0:T(8,128)} %param.21) | copy-start | bytes 786436
  0.0 104.4 %collective-permute-start.1 = (f32[16,4096]{1,0:T(8,128)}, f32[16,4096]{1,0:T(8,128)S(1)}, u32[]{:S(2)}, u32[]{:S(2)}) collective-permute-start(f32[16,4096]{1,0:T(8,128)} %param.14), channel_id=1, source_target_pairs={{1,0},{2,1},{3,2},{4,3},{5,4},{6,5},{7,6},{8,7},{9,8},{10,9},{11,1... | collective-permute-start | bytes 786440 | tf_op jit(solution)/shard_map/ppermute | solution.py:24
  1.4 102.9 %collective-permute-start = (f32[16,4096]{1,0:T(8,128)}, f32[16,4096]{1,0:T(8,128)}, u32[]{:S(2)}, u32[]{:S(2)}) collective-permute-start(f32[16,4096]{1,0:T(8,128)} %param.14), channel_id=1, source_target_pairs={{0,1},{1,2},{2,3},{3,4},{4,5},{5,6},{6,7},{7,8},{8,9},{9,10},{10,1... | collective-permute-start | bytes 786440 | tf_op jit(solution)/shard_map/ppermute | solution.py:23
  7.8 34.0 %copy-start = (f32[64,32,64]{2,1,0:T(8,128)}, f32[64,32,64]{2,1,0:T(8,128)S(1)}, u32[]{:S(2)}) copy-start(f32[64,32,64]{2,1,0:T(8,128)S(1)} %reshape.72) | copy-start | bytes 1572868
  7.8 32.8 %copy-start.7 = (s32[4,8]{1,0:T(4,128)S(1)}, s32[4,8]{1,0:T(4,128)}, u32[]{:S(2)}) copy-start(s32[4,8]{1,0:T(4,128)} %param.22) | copy-start | bytes 388
  9.8 33.1 %copy-start.3 = (f32[4,1024]{1,0:T(4,128)S(1)}, f32[4,1024]{1,0:T(4,128)}, u32[]{:S(2)}) copy-start(f32[4,1024]{1,0:T(4,128)} %param.24) | copy-start | bytes 49156
  9.8 57.8 %copy-start.4 = (f32[1,4,1024]{2,1,0:T(4,128)S(1)}, f32[1,4,1024]{2,1,0:T(4,128)}, u32[]{:S(2)}) copy-start(f32[1,4,1024]{2,1,0:T(4,128)} %param.25) | copy-start | bytes 49156
  9.8 57.9 %copy-start.5 = (s32[64,8]{0,1:T(8,128)S(1)}, s32[64,8]{0,1:T(8,128)}, u32[]{:S(2)}) copy-start(s32[64,8]{0,1:T(8,128)} %param.19) | copy-start | bytes 6148
  10.0 60.2 %copy-start.6 = (s32[64,8]{0,1:T(8,128)S(1)}, s32[64,8]{0,1:T(8,128)}, u32[]{:S(2)}) copy-start(s32[64,8]{0,1:T(8,128)} %param.16) | copy-start | bytes 6148
  10.9 73.2 %collective-permute-start.3 = (f32[16,2048]{1,0:T(8,128)}, f32[16,2048]{1,0:T(8,128)}, u32[]{:S(2)}, u32[]{:S(2)}) collective-permute-start(f32[16,2048]{1,0:T(8,128)} %reshape.74), channel_id=1, source_target_pairs={{1,0},{2,1},{3,2},{4,3},{5,4},{6,5},{7,6},{8,7},{9,8},{10,9},{11,1... | collective-permute-start | bytes 393224 | tf_op jit(solution)/shard_map/ppermute | solution.py:24
  12.2 74.1 %collective-permute-start.2 = (f32[16,2048]{1,0:T(8,128)}, f32[16,2048]{1,0:T(8,128)}, u32[]{:S(2)}, u32[]{:S(2)}) collective-permute-start(f32[16,2048]{1,0:T(8,128)} %reshape.74), channel_id=1, source_target_pairs={{0,1},{1,2},{2,3},{3,4},{4,5},{5,6},{6,7},{7,8},{8,9},{9,10},{10,1... | collective-permute-start | bytes 393224 | tf_op jit(solution)/shard_map/ppermute | solution.py:23
  74.0 9.4 %copy-start.8 = (s32[64]{0:T(128)S(1)}, s32[64]{0:T(128)}, u32[]{:S(2)}) copy-start(s32[64]{0:T(128)} %param.17) | copy-start | bytes 772
  91.9 12.5 %copy-start.1 = (f32[16,4096]{1,0:T(8,128)S(1)}, f32[16,4096]{1,0:T(8,128)}, u32[]{:S(2)}) copy-start(f32[16,4096]{1,0:T(8,128)} %param.14) | copy-start | bytes 786436
where the time goes:
time: 225 us; the launch traced here: 224 us
  local copies, waits for them, and re-layouts  95.1 us (42%)
  matrix products  63.5 us (28%)
  blocking collectives  44.3 us (20%)
  starting transfers between devices  11.6 us (5%)
  loops' own time  5.86 us (3%)
  other arithmetic  3.04 us (1%)
    dot_general x8, matrix products, near_step(): term = jnp.einsum('tab,trb->tra', slab, picked, precision=highest_precision)  42 us
    dynamic_slice x16, local copies, waits for them, and re-layouts, near_step(): lax.dynamic_index_in_dim(near_blocks, slot_index, axis=1, keepdims=False)  40.3 us
    all_gather x1, blocking collectives, per_device(): shard_rows = lax.all_gather(cluster_rows, 'leaf', axis=0, tiled=True)  20.1 us
    gather x8, local copies, waits for them, and re-layouts, near_step(): picked = jnp.take(point_blocks, near_local[:, slot_index], axis=0)  16 us
    psum x1, blocking collectives, per_device(): group_sum = lax.psum(projected_sum, 'leaf')  14.1 us
    dot_general x1, matrix products, per_device(): jnp.einsum('tjkl,rtjl->tkr', leaf_coupling.reshape(leaves_here, FAR0, K,...  10.6 us
    all_gather x1, blocking collectives, per_device(): all_groups = lax.all_gather(group_sum, 'group', axis=0, tiled=True)  10 us
    reshape x1, local copies, waits for them, and re-layouts, per_device(): leaf_coupling.reshape(leaves_here, FAR0, K, K)  9.12 us
  transfers between devices with their start and end apart: 4, of which 0 were waited for; matrix products, arithmetic and copies ran while one was open for 22% of the time, Pallas kernels for 0%

commit v1 on v0

v1 whole, which is shorter than its diff:
```python
import functools

import jax
import jax.numpy as jnp
from jax import lax
from jax.experimental import pallas as pl
from jax.experimental.pallas import tpu as pltpu
from jax.sharding import PartitionSpec as P

LEAF = 64
K = 32
RHS = 16
FAR0 = 8
FAR1 = 8
NEAR = 8
LANES = 128
KR = K * RHS
KK = K * K
CHUNK = 8

f32 = jnp.float32
bf16 = jnp.bfloat16
MESH = pl.DeviceIdType.MESH
VMEM = pl.BlockSpec(memory_space=pltpu.VMEM)
SMEM = pl.BlockSpec(memory_space=pltpu.SMEM)
NT = (((1,), (1,)), ((), ()))
NN = (((1,), (0,)), ((), ()))


def halves(value):
    high = value.astype(bf16)
    low = (value - high.astype(f32)).astype(bf16)
    return high, low


def mm(a, b, dims=NN):
    return lax.dot_general(a, b, dims, preferred_element_type=f32)


def pick(value, chosen):
    high, low = halves(value)
    return mm(high, chosen) + mm(low, chosen)


def iota(shape, dim):
    return lax.broadcasted_iota(jnp.int32, shape, dim)


def mask(condition):
    return jnp.where(condition, 1.0, 0.0).astype(bf16)


def doubled_pair(pair):
    first = iota(pair.shape, 1) < LEAF
    turned = pltpu.roll(pair, LEAF, 1)
    zero = jnp.zeros_like(pair)
    even = jnp.concatenate([jnp.where(first, pair, zero), jnp.where(first, zero, turned)], axis=0)
    odd = jnp.concatenate([jnp.where(first, turned, zero), jnp.where(first, zero, pair)], axis=0)
    return even, odd


def coef_kernel(x_ref, basis_ref, coef_ref):
    def step(p, carry):
        pair = x_ref[:, pl.ds(pl.multiple_of(p * LANES, LANES), LANES)]
        for side, doubled in enumerate(doubled_pair(pair)):
            xh, xl = halves(doubled)
            bh, bl = halves(basis_ref[2 * p + side])
            both = jnp.concatenate([bh, bl], axis=1)
            twice = jnp.concatenate([xh, xh], axis=1)
            coef_ref[2 * p + side] = mm(both, twice, NT) + mm(bh, xl, NT)
        return carry

    lax.fori_loop(0, basis_ref.shape[0] // 2, step, 0, unroll=4)


def turn(src, rows, dst_ref, lane):
    here = min(LANES, src.shape[0] - rows)
    for c in range(src.shape[1] // LANES):
        block = src[rows : rows + here, c * LANES : (c + 1) * LANES]
        if here < LANES:
            block = jnp.concatenate([block, jnp.zeros((LANES - here, LANES), f32)], axis=0)
        dst_ref[c * LANES : (c + 1) * LANES, lane : lane + LANES] = block.T


def small_products(at_ref, g_ref, out_ref, tiles, transposed=False):
    width = 8

    def step(i, carry):
        tile, kb = i // (K // width), i % (K // width)
        lanes = pl.ds(pl.multiple_of(tile * LANES, LANES), LANES)
        acc = [jnp.zeros((RHS, LANES), f32)] * width
        for l8 in range(0, K, 8):
            if transposed:
                at = [at_ref[pl.ds(pl.multiple_of(kb * 8, 8) + l * K, 8), lanes] for l in range(l8, l8 + 8)]
            else:
                at = [at_ref[pl.ds(pl.multiple_of(kb * 8 * K, 8 * K) + j * K + l8, 8), lanes] for j in range(width)]
            for i in range(8):
                g = g_ref[(l8 + i) * RHS : (l8 + i + 1) * RHS, lanes]
                for j in range(width):
                    row = at[i][j : j + 1] if transposed else at[j][i : i + 1]
                    acc[j] = acc[j] + row * g
        for j in range(width):
            start = pl.multiple_of(kb * (width * RHS) + j * RHS, RHS)
            out_ref[pl.ds(start, RHS), lanes] = acc[j]
        return carry

    lax.fori_loop(0, tiles * (K // width), step, 0)


def up_kernel(base, cpd, coef_ref, transfer_ref, small_ref, out_ref, et, ct, st, work):
    leaves = coef_ref.shape[0]
    per = leaves // cpd
    turn(coef_ref, 0, ct, 0)
    turn(transfer_ref, 0, et, 0)
    turn(small_ref, 0, st, 0)
    small_products(et, ct, work, 1)
    t, q = iota((LANES, LANES), 0), iota((LANES, LANES), 1)
    chosen = mask((q - base == t // per) & (t < leaves))
    ct[...] = pick(work[...], chosen)
    small_products(st, ct, work, 1)
    for c in range(KR // LANES):
        rows = slice(c * LANES, (c + 1) * LANES)
        out_ref[0:8, rows] = ct[rows, :].T[base : base + 8]
        total = jnp.sum(work[rows, :].T[base : base + cpd], axis=0, keepdims=True)
        out_ref[8:16, rows] = jnp.broadcast_to(total, (8, LANES))


def down_kernel(base, cpd, groups, coef_ref, near_coef_ref, transfer_ref, coupling_ref, small_ref, cluster_ref, group_ref,
                leaf_idx_ref, cluster_idx_ref, field_ref, et, ct, st, lt, gt, gl, work, lwork, small_g):
    leaves = transfer_ref.shape[0]
    per = leaves // cpd
    slots = leaves * FAR0
    turn(transfer_ref, 0, et, 0)
    turn(small_ref, 0, st, 0)
    for tile in range(slots // LANES):
        turn(coupling_ref, tile * LANES, lt, tile * LANES)
    for part in range(-(-coef_ref.shape[0] // LANES)):
        turn(coef_ref, part * LANES, ct, part * LANES)
    sources = ct.shape[1]
    onehot = mask(iota((sources, slots), 0) == leaf_idx_ref[...])
    gl[...] = pick(ct[...], onehot)
    small_products(lt, gl, lwork, slots // LANES)
    rows = cluster_ref.shape[0]
    count = gt.shape[1]
    for part in range(count // LANES):
        if part * LANES < rows:
            turn(cluster_ref, part * LANES, gt, part * LANES)
        else:
            turn(group_ref, 0, gt, part * LANES)
    onehot = mask(iota((count, LANES), 0) == cluster_idx_ref[...])
    small_g[...] = pick(gt[...], onehot)
    small_products(st, small_g, work, 1)
    a, b = iota((LANES, LANES), 0), iota((LANES, LANES), 1)
    wide = cpd * FAR1
    mine = (b >= base) & (b < base + cpd)
    top = mask((a >= wide) & (a < wide + groups) & mine)
    small_g[...] = pick(work[...], top)
    slot = mask((a < wide) & (b - base == a // FAR1))
    far = pick(work[...], slot)
    small_products(st, small_g, work, 1, transposed=True)
    spread = mask((a - base == b // per) & (b < leaves))
    small_g[...] = pick(far + work[...], spread)
    small_products(et, small_g, work, 1, transposed=True)
    gather = mask(iota((slots, LANES), 0) // FAR0 == iota((slots, LANES), 1))
    field = work[...] + pick(lwork[...], gather)
    for c in range(KR // LANES):
        rows_c = slice(c * LANES, (c + 1) * LANES)
        field_ref[:, rows_c] = field[rows_c].T[:leaves]


def near_kernel(idx_ref, near_ref, before_ref, own_ref, after_ref, basis_ref, field_ref, out_ref, xh_ref, xl_ref, place_ref, part_ref):
    chunk = pl.program_id(0)
    leaves = own_ref.shape[1] // LEAF

    @pl.when(chunk == 0)
    def _():
        for part, ref in enumerate((before_ref, own_ref, after_ref)):

            def build(p, carry, ref=ref, part=part):
                pair = ref[:, pl.ds(pl.multiple_of(p * LANES, LANES), LANES)]
                for side, doubled in enumerate(doubled_pair(pair)):
                    high, low = halves(doubled)
                    xh_ref[part * leaves + 2 * p + side] = high
                    xl_ref[part * leaves + 2 * p + side] = low
                return carry

            lax.fori_loop(0, leaves // 2, build, 0, unroll=4)
        xh_ref[3 * leaves] = jnp.zeros(xh_ref.shape[1:], bf16)
        xl_ref[3 * leaves] = jnp.zeros(xl_ref.shape[1:], bf16)
        row, col = iota((2 * LANES, LANES), 0), iota((2 * LANES, LANES), 1)
        for side in range(2):
            for half in range(2):
                place_ref[2 * side + half] = mask(col == side * LEAF + 2 * (row // NEAR) + half)

    slot_of_lane = iota((2 * RHS, 2 * LANES), 1) % NEAR
    for i in range(CHUNK):
        n = near_ref[i]
        rows = jnp.concatenate([n[:, c * LANES : (c + 1) * LANES] for c in range(LEAF // 2)], axis=0)
        nh, nl = halves(rows)
        weights = jnp.concatenate([nh, nl], axis=1)
        at = [idx_ref[(chunk * CHUNK + i) * NEAR + j] for j in range(NEAR)]
        xh = jnp.concatenate([xh_ref[s] for s in at], axis=0)
        xl = jnp.concatenate([xl_ref[s] for s in at], axis=0)
        full = mm(jnp.concatenate([xh, xh], axis=1), weights, NT) + mm(
            jnp.concatenate([xl, xl], axis=1), weights, NT
        )
        kept = full[: 2 * RHS]
        for j in range(1, NEAR):
            kept = jnp.where(slot_of_lane == j, full[j * 2 * RHS : (j + 1) * 2 * RHS], kept)
        part_ref[i] = kept

    total = jnp.zeros((CHUNK // 2 * RHS, LANES), f32)
    for side in range(2):
        for half in range(2):
            rows = jnp.concatenate(
                [part_ref[2 * p + side, half * RHS : (half + 1) * RHS] for p in range(CHUNK // 2)], axis=0
            )
            total = total + pick(rows, place_ref[2 * side + half])

    first = iota((RHS, LANES), 1) < LEAF
    for p in range(CHUNK // 2):
        ends = []
        for side in range(2):
            i = 2 * p + side
            fh, fl = halves(field_ref[i])
            bh, bl = halves(basis_ref[i])
            wide = mm(jnp.concatenate([fh, fl], axis=0), jnp.concatenate([bh, bl], axis=1))
            both = wide[: 2 * RHS, :LANES] + wide[: 2 * RHS, LANES:] + wide[2 * RHS :, :LANES]
            ends.append((both[:RHS], both[RHS:]))
        straight = jnp.where(first, ends[0][0], ends[1][1])
        crossed = jnp.where(first, ends[1][0], ends[0][1])
        out_ref[:, p * LANES : (p + 1) * LANES] = (
            total[p * RHS : (p + 1) * RHS] + straight + pltpu.roll(crossed, LEAF, 1)
        )


def exchange_kernel(nleaf, ngroup, block_ref, gathered_ref, group_ref, sums, leaf_send, leaf_recv, group_send, group_recv):
    g, z = lax.axis_index("group"), lax.axis_index("leaf")
    barrier = pltpu.get_barrier_semaphore()

    def greet_leaf(d, carry):
        pl.semaphore_signal(barrier, inc=1, device_id=(g, lax.rem(z + d, nleaf)), device_id_type=MESH)
        return carry

    def greet_group(d, carry):
        pl.semaphore_signal(barrier, inc=1, device_id=(lax.rem(g + d, ngroup), z), device_id_type=MESH)
        return carry

    lax.fori_loop(1, nleaf, greet_leaf, 0)
    lax.fori_loop(1, ngroup, greet_group, 0)
    pl.semaphore_wait(barrier, nleaf + ngroup - 2)

    def to_leaf(d):
        peer = lax.rem(z + d, nleaf)
        return pltpu.make_async_remote_copy(
            src_ref=block_ref, dst_ref=gathered_ref.at[z], send_sem=leaf_send.at[d], recv_sem=leaf_recv.at[z],
            device_id=(g, peer), device_id_type=MESH)

    def from_leaf(d):
        peer = lax.rem(z + d, nleaf)
        return pltpu.make_async_remote_copy(
            src_ref=block_ref, dst_ref=gathered_ref.at[peer], send_sem=leaf_send.at[d], recv_sem=leaf_recv.at[peer],
            device_id=(g, peer), device_id_type=MESH)

    def start_leaf(d, carry):
        to_leaf(d).start()
        return carry

    lax.fori_loop(1, nleaf, start_leaf, 0)
    gathered_ref[z] = block_ref[...]

    def wait_leaf(d, carry):
        from_leaf(d).wait()
        return carry

    lax.fori_loop(1, nleaf, wait_leaf, 0)

    def add(i, total):
        return total + gathered_ref[i, 8:16]

    total = lax.fori_loop(0, nleaf, add, jnp.zeros((8, KR), f32))
    sums[...] = total
    group_ref[g] = total

    def group_copy(d, slot):
        peer = lax.rem(g + d, ngroup)
        at = g if slot else peer
        return pltpu.make_async_remote_copy(
            src_ref=sums, dst_ref=group_ref.at[at], send_sem=group_send.at[d], recv_sem=group_recv.at[at],
            device_id=(peer, z), device_id_type=MESH)

    for d in range(1, ngroup):
        group_copy(d, True).start()
    for d in range(1, ngroup):
        group_copy(d, False).wait()


def params(**kw):
    return pltpu.CompilerParams(vmem_limit_bytes=48 * 1024 * 1024, **kw)


def per_device(
    right_sides,
    near_blocks,
    near_source,
    near_count,
    basis,
    leaf_source,
    leaf_coupling,
    leaf_transfer,
    cluster_source,
    cluster_coupling,
    cluster_transfer,
    group_coupling,
):
    leaves = near_blocks.shape[0]
    cpd = cluster_coupling.shape[0]
    ngroup, nleaf = lax.axis_size("group"), lax.axis_size("leaf")
    device = lax.axis_index(("group", "leaf"))
    window_start = (device - 1) * leaves
    axes = ("group", "leaf")
    size = ngroup * nleaf
    up = [(i, i + 1) for i in range(size - 1)]
    down = [(j, i) for i, j in up]

    x_before = lax.ppermute(right_sides, axes, up)
    x_after = lax.ppermute(right_sides, axes, down)

    basis3 = basis.reshape(leaves, K * LEAF // LANES, LANES)
    coef = pl.pallas_call(
        coef_kernel,
        out_shape=jax.ShapeDtypeStruct((leaves, K // 2, 2 * RHS), f32),
        in_specs=[VMEM, VMEM],
        out_specs=VMEM,
        compiler_params=params(),
        name="leaf_coefficients",
    )(right_sides, basis3)
    coef = coef.reshape(leaves, KR)
    coef_before = lax.ppermute(coef, axes, up)
    coef_after = lax.ppermute(coef, axes, down)

    wide = cpd * FAR1
    base = wide + 8
    assert ngroup <= 8 and cpd <= 8 and base + 8 <= LANES and leaves <= LANES
    small = jnp.concatenate(
        [
            cluster_coupling.reshape(wide, KK),
            jnp.pad(group_coupling.reshape(ngroup, KK), ((0, 8 - ngroup), (0, 0))),
            jnp.pad(cluster_transfer, ((0, 8 - cpd), (0, 0))),
        ],
        axis=0,
    )
    block = pl.pallas_call(
        functools.partial(up_kernel, base, cpd),
        out_shape=jax.ShapeDtypeStruct((16, KR), f32),
        in_specs=[VMEM] * 3,
        out_specs=VMEM,
        scratch_shapes=[
            pltpu.VMEM((KK, LANES), f32),
            pltpu.VMEM((KR, LANES), f32),
            pltpu.VMEM((KK, LANES), f32),
            pltpu.VMEM((KR, LANES), f32),
        ],
        compiler_params=params(),
        name="to_clusters",
    )(coef, leaf_transfer, small)

    gathered, group_sums = pl.pallas_call(
        functools.partial(exchange_kernel, nleaf, ngroup),
        out_shape=(
            jax.ShapeDtypeStruct((nleaf, 16, KR), f32),
            jax.ShapeDtypeStruct((ngroup, 8, KR), f32),
        ),
        in_specs=[VMEM],
        out_specs=(VMEM, VMEM),
        scratch_shapes=[
            pltpu.VMEM((8, KR), f32),
            pltpu.SemaphoreType.DMA((nleaf,)),
            pltpu.SemaphoreType.DMA((nleaf,)),
            pltpu.SemaphoreType.DMA((ngroup,)),
            pltpu.SemaphoreType.DMA((ngroup,)),
        ],
        compiler_params=params(collective_id=0, has_side_effects=True),
        name="exchange",
    )(block)

    rows = nleaf * 16
    padded = -(-rows // LANES) * LANES
    source_row = cluster_source // cpd * 16 + cluster_source % cpd
    cluster_idx = jnp.concatenate(
        [
            source_row.reshape(1, wide),
            padded + 8 * jnp.arange(ngroup, dtype=jnp.int32).reshape(1, ngroup),
            jnp.full((1, LANES - wide - ngroup), -1, jnp.int32),
        ],
        axis=1,
    )
    leaf_idx = (leaf_source - window_start).reshape(1, leaves * FAR0)
    coef_ext = jnp.concatenate([coef_before, coef, coef_after], axis=0)
    source_lanes = -(-3 * leaves // LANES) * LANES
    field = pl.pallas_call(
        functools.partial(down_kernel, base, cpd, ngroup),
        out_shape=jax.ShapeDtypeStruct((leaves, KR), f32),
        in_specs=[VMEM] * 9,
        out_specs=VMEM,
        scratch_shapes=[
            pltpu.VMEM((KK, LANES), f32),
            pltpu.VMEM((KR, source_lanes), f32),
            pltpu.VMEM((KK, LANES), f32),
            pltpu.VMEM((KK, leaves * FAR0), f32),
            pltpu.VMEM((KR, padded + LANES), f32),
            pltpu.VMEM((KR, leaves * FAR0), f32),
            pltpu.VMEM((KR, LANES), f32),
            pltpu.VMEM((KR, leaves * FAR0), f32),
            pltpu.VMEM((KR, LANES), f32),
        ],
        compiler_params=params(),
        name="from_clusters",
    )(
        coef_ext,
        coef,
        leaf_transfer,
        leaf_coupling.reshape(leaves * FAR0, KK),
        small,
        gathered.reshape(rows, KR),
        group_sums.reshape(ngroup * 8, KR),
        leaf_idx,
        cluster_idx,
    )
    field = field.reshape(leaves, K // 2, 2 * RHS).transpose(0, 2, 1)

    live = jnp.arange(NEAR, dtype=jnp.int32)[None, :] < near_count[:, None]
    near_idx = jnp.where(live, near_source - window_start, 3 * leaves).reshape(leaves * NEAR)
    whole = pl.BlockSpec((RHS, leaves * LEAF), lambda i: (0, 0))
    return pl.pallas_call(
        near_kernel,
        grid=(leaves // CHUNK,),
        out_shape=jax.ShapeDtypeStruct((RHS, leaves * LEAF), f32),
        in_specs=[
            SMEM,
            pl.BlockSpec((CHUNK, NEAR, LEAF * LEAF), lambda i: (i, 0, 0)),
            whole,
            whole,
            whole,
            pl.BlockSpec((CHUNK, K * LEAF // LANES, LANES), lambda i: (i, 0, 0)),
            pl.BlockSpec((CHUNK, 2 * RHS, K // 2), lambda i: (i, 0, 0)),
        ],
        out_specs=pl.BlockSpec((RHS, CHUNK * LEAF), lambda i: (0, i)),
        scratch_shapes=[
            pltpu.VMEM((3 * leaves + 1, 2 * RHS, LANES), bf16),
            pltpu.VMEM((3 * leaves + 1, 2 * RHS, LANES), bf16),
            pltpu.VMEM((4, 2 * LANES, LANES), bf16),
            pltpu.VMEM((CHUNK, 2 * RHS, 2 * LANES), f32),
        ],
        compiler_params=params(),
        name="near_and_sum",
    )(near_idx, near_blocks, x_before, right_sides, x_after, basis3, field)


def solution(mesh):
    split = P(("group", "leaf"))
    in_specs = (
        P(None, ("group", "leaf")),
        split,
        split,
        split,
        split,
        split,
        split,
        split,
        split,
        split,
        split,
        P("group"),
    )
    return jax.shard_map(
        per_device, mesh=mesh, in_specs=in_specs, out_specs=P(None, ("group", "leaf")), check_vma=False
    )
```

time: 225 us -> 68.1 us (0.30)
  local copies, waits for them, and re-layouts: 95.1 us -> 7.47 us
  matrix products: 63.5 us -> 0 us
  Pallas kernels: 0 us -> 46.4 us
  blocking collectives: 44.3 us -> 0 us
  loops' own time: 5.86 us -> 0 us
    dot_general x18 -> x0, matrix products: 63.5 us -> none  [the longest x8 42 us: near_step(): term = jnp.einsum('tab,trb->tra', slab, picked, precision=highest_precision)]
    pallas_call x0 -> x5, Pallas kernels: none -> 46.4 us  [the longest x1 20.8 us: per_device(): pl.pallas_call(functools.partial(exchange_kernel, nleaf, ngroup), out_sha...]
    dynamic_slice x16 -> x0, local copies, waits for them, and re-layouts: 40.3 us -> none  [near_step(): lax.dynamic_index_in_dim(near_blocks, slot_index, axis=1, keepdims=False)]
    all_gather x2 -> x0, blocking collectives: 30.1 us -> none  [the longest x1 20.1 us: per_device(): shard_rows = lax.all_gather(cluster_rows, 'leaf', axis=0, tiled=True)]
    reshape x21 -> x5, local copies, waits for them, and re-layouts: 24.1 us -> 1.33 us  [the longest x1 0.95 us: per_device(): field = field.reshape(leaves, K // 2, 2 * RHS).transpose(0, 2, 1)]
    gather x9 -> x0, local copies, waits for them, and re-layouts: 19.1 us -> none  [the longest x8 16 us: near_step(): picked = jnp.take(point_blocks, near_local[:, slot_index], axis=0)]
    psum x1 -> x0, blocking collectives: 14.1 us -> none  [per_device(): group_sum = lax.psum(projected_sum, 'leaf')]
    another operation x1 -> x0, loops' own time: 5.86 us -> none  [per_device(): lax.fori_loop(0, busiest, near_step, jnp.zeros((leaves_here, RHS, LEAF),...]
  transfers between devices with their start and end apart: 4 -> 4, of which waited for: 0 -> 0; matrix products, arithmetic and copies ran while one was open for 22% -> 8% of each run, Pallas kernels for 0% -> 49%
where the time goes in v1:
time: 68.1 us; the launch traced here: 67.5 us
  Pallas kernels  46.4 us (68%)
  starting transfers between devices  10.9 us (16%)
  local copies, waits for them, and re-layouts  7.47 us (11%)
  other arithmetic  2.49 us (4%)
    pallas_call x1, Pallas kernels, per_device(): pl.pallas_call(functools.partial(exchange_kernel, nleaf, ngroup), out_sha...  20.8 us
    pallas_call x1, Pallas kernels, per_device(): pl.pallas_call(near_kernel, grid=(leaves // CHUNK,), out_shape=jax.ShapeD...  13.2 us
    pallas_call x1, Pallas kernels, per_device(): pl.pallas_call(functools.partial(down_kernel, base, cpd, ngroup), out_sha...  8.2 us
    unnamed x11, local copies, waits for them, and re-layouts  5.57 us
    ppermute x1, starting transfers between devices, per_device(): coef_before = lax.ppermute(coef, axes, up)  5.17 us
    ppermute x1, starting transfers between devices, per_device(): x_before = lax.ppermute(right_sides, axes, up)  3.05 us
    pallas_call x1, Pallas kernels, per_device(): pl.pallas_call(functools.partial(up_kernel, base, cpd), out_shape=jax.Sha...  2.12 us
    pallas_call x1, Pallas kernels, per_device(): pl.pallas_call(coef_kernel, out_shape=jax.ShapeDtypeStruct((leaves, K //...  2.08 us
  transfers between devices with their start and end apart: 4, of which 0 were waited for; matrix products, arithmetic and copies ran while one was open for 8% of the time, Pallas kernels for 49%

profile of v1, /device:TPU:0, one launch (start us, length us, event | category | flops | bytes accessed | tf_op | source)
XLA Modules:
  0.0 67.5 jit_solution(5774933976493582707)
XLA Ops:
  0.0 0.0 copy-start.2
  0.0 1.4 %collective-permute-start.1 = (f32[16,4096]{1,0:T(8,128)}, f32[16,4096]{1,0:T(8,128)S(1)}, u32[]{:S(2)}, u32[]{:S(2)}) collective-permute-start(f32[16,4096]{1,0:T(8,128)} %own_ref.1), channel_id=1, source_target_pairs={{1,0},{2,1},{3,2},{4,3},{5,4},{6,5},{7,6},{8,7},{9,8},{10,9},{11,1... | collective-permute-start | bytes 786440 | tf_op jit(solution)/shard_map/ppermute | solution.py:327
  1.4 3.1 %collective-permute-start = (f32[16,4096]{1,0:T(8,128)}, f32[16,4096]{1,0:T(8,128)S(1)}, u32[]{:S(2)}, u32[]{:S(2)}) collective-permute-start(f32[16,4096]{1,0:T(8,128)} %own_ref.1), channel_id=1, source_target_pairs={{0,1},{1,2},{2,3},{3,4},{4,5},{5,6},{6,7},{7,8},{8,9},{9,10},{10,1... | collective-permute-start | bytes 786440 | tf_op jit(solution)/shard_map/ppermute | solution.py:326
  4.5 1.1 %copy.24 = f32[8,8,16,128]{3,2,1,0:T(8,128)S(1)} copy(f32[8,8,16,128]{3,1,2,0:T(8,128)} %bitcast.20) | data formatting | bytes 1048576
  5.6 0.0 copy-start.1
  5.6 0.9 %copy-done.1 = f32[16,4096]{1,0:T(8,128)S(1)} copy-done((f32[16,4096]{1,0:T(8,128)S(1)}, f32[16,4096]{1,0:T(8,128)}, u32[]{:S(2)}) %copy-start.1) | copy-done | bytes 262168
  6.6 2.1 %leaf_coefficients.1 = f32[64,16,32]{2,1,0:T(8,128)S(1)} custom-call(f32[16,4096]{1,0:T(8,128)S(1)} %copy-done.1, f32[64,16,128]{2,1,0:T(8,128)S(1)} %bitcast.12), custom_call_target="tpu_custom_call" | custom-call | tf_op jit(solution)/shard_map/leaf_coefficients/pallas_call | solution.py:330
  8.7 0.3 copy.15
  8.9 0.1 copy.16.coef_ref.near_coef_ref
  9.0 1.3 %collective-permute-start.3 = (f32[64,512]{1,0:T(8,128)S(1)}, f32[64,512]{1,0:T(8,128)S(1)}, u32[]{:S(2)}, u32[]{:S(2)}) collective-permute-start(f32[64,512]{1,0:T(8,128)S(1)} %copy.16.coef_ref.near_coef_ref), channel_id=1, source_target_pairs={{1,0},{2,1},{3,2},{4,3},{5,4},{6,5},{7,6},{8,7},{9,8},{10,9},{11,1... | collective-permute-start | bytes 393224 | tf_op jit(solution)/shard_map/ppermute | solution.py:340
  10.3 5.2 %collective-permute-start.2 = (f32[64,512]{1,0:T(8,128)S(1)}, f32[64,512]{1,0:T(8,128)S(1)}, u32[]{:S(2)}, u32[]{:S(2)}) collective-permute-start(f32[64,512]{1,0:T(8,128)S(1)} %copy.16.coef_ref.near_coef_ref), channel_id=1, source_target_pairs={{0,1},{1,2},{2,3},{3,4},{4,5},{5,6},{6,7},{7,8},{8,9},{9,10},{10,1... | collective-permute-start | bytes 393224 | tf_op jit(solution)/shard_map/ppermute | solution.py:339
  15.5 0.7 %fusion.2 = s32[4,8]{1,0:T(4,128)S(1)} fusion(s32[4,8]{1,0:T(4,128)} %param.20), kind=kLoop, calls=%fused_computation.15 | loop fusion | flops 672 | bytes 256 | tf_op jit(solution)/shard_map/add | solution.py:389
  16.2 1.0 %select_maximum_fusion.small_ref = f32[48,1024]{1,0:T(8,128)S(1)} fusion(f32[4,1024]{1,0:T(4,128)} %param.22, f32[4,1024]{1,0:T(4,128)} %bitcast.22, f32[32,1024]{1,0:T(8,128)} %bitcast.21), kind=kLoop, calls=%fused_computation.3 | loop fusion | flops 393216 | bytes 360448 | tf_op jit(solution)/shard_map/concatenate | solution.py:345
  17.2 0.7 %subtract_select_fusion = (s32[64,8]{0,1:T(8,128)S(1)}, s32[64,8]{0,1:T(8,128)S(1)}) fusion(s32[64,8]{0,1:T(8,128)} %param.14, s32[]{:T(128)S(6)} %mul.24, s32[64]{0:T(128)} %param.15, s32[64,8]{0,1:T(8,128)} %param.17), kind=kLoop, calls=%fused_computation.7 | loop fusion | flops 2048 | bytes 8452 | tf_op jit(solution)/shard_map/jit(_where)/select_n | solution.py:433
  17.9 0.1 reshape.56
  18.0 0.1 copy.14
  18.1 0.1 reshape.47.idx_ref
  18.2 0.1 copy.20
  18.3 0.1 reshape.55.leaf_idx_ref
  18.4 0.0 copy-start.3
  18.4 0.9 %copy-done.3 = f32[64,1024]{1,0:T(8,128)S(1)} copy-done((f32[64,1024]{1,0:T(8,128)S(1)}, f32[64,1024]{1,0:T(8,128)}, u32[]{:S(2)}) %copy-start.3) | copy-done | bytes 262168
  19.3 2.1 %to_clusters.1.block_ref = f32[16,512]{1,0:T(8,128)S(1)} custom-call(f32[64,512]{1,0:T(8,128)S(1)} %copy.16.coef_ref.near_coef_ref, f32[64,1024]{1,0:T(8,128)S(1)} %copy-done.3, f32[48,1024]{1,0:T(8,128)S(1)} %select_maximum_fusion.small_ref), custom_call_target="tpu_custom_call" | custom-call | tf_op jit(solution)/shard_map/to_clusters/pallas_call | solution.py:353
  21.4 20.8 %exchange.1 = (f32[8,16,512]{2,1,0:T(8,128)S(1)}, f32[4,8,512]{2,1,0:T(8,128)S(1)}) custom-call(f32[16,512]{1,0:T(8,128)S(1)} %to_clusters.1.block_ref), custom_call_target="tpu_custom_call" | custom-call | tf_op jit(solution)/shard_map/exchange/pallas_call | solution.py:368
  42.3 0.1 bitcast_add_fusion.cluster_idx_ref
  42.4 0.0 collective-permute-done.3
  42.4 0.0 collective-permute-done.2
  42.4 0.0 copy-start
  42.4 1.6 %copy-done = f32[64,8,1024]{2,1,0:T(8,128)S(1)} copy-done((f32[64,8,1024]{2,1,0:T(8,128)S(1)}, f32[64,8,1024]{2,1,0:T(8,128)}, u32[]{:S(2)}) %copy-start) | copy-done | bytes 2097176
  44.0 0.0 copy-start.4
  44.0 0.9 %copy-done.4 = f32[64,1024]{1,0:T(8,128)S(1)} copy-done((f32[64,1024]{1,0:T(8,128)S(1)}, f32[64,1024]{1,0:T(8,128)}, u32[]{:S(2)}) %copy-start.4) | copy-done | bytes 262168
  45.0 8.2 %from_clusters.1 = f32[64,512]{1,0:T(8,128)S(1)} custom-call(f32[192,512]{1,0:T(8,128)S(1)} %pad_maximum_fusion.coef_ref, f32[64,512]{1,0:T(8,128)S(1)} %copy.16.coef_ref.near_coef_ref, f32[64,1024]{1,0:T(8,128)S(1)} %copy-done.4, f32[512,1024]{1,0:T(8,128)S(1)} %bitcast.15, f32[48,1024]{1,0:T(8,128)S(1)} %select_maximum_fusion.small_ref, ...), custom_call_target="tpu_custom_call" | custom-call | tf_op jit(solution)/shard_map/from_clusters/pallas_call | solution.py:401
  53.2 0.1 copy.22
  53.3 1.0 %copy.23 = f32[64,16,32]{1,2,0:T(8,128)S(1)} copy(f32[64,16,32]{0,2,1:T(8,128)S(1)} %bitcast.19) | data formatting | bytes 262144 | tf_op jit(solution)/shard_map/reshape | solution.py:430
  54.3 0.0 collective-permute-done.1.after_ref
  54.3 0.0 collective-permute-done.before_ref
  54.3 0.0 copy-done.2
  54.3 13.2 %near_and_sum.1 = f32[16,4096]{1,0:T(8,128)} custom-call(s32[512]{0:T(512)S(1)} %reshape.47.idx_ref, f32[64,8,4096]{2,1,0:T(8,128)} %near_ref.1, f32[16,4096]{1,0:T(8,128)S(1)} %collective-permute-done.before_ref, f32[16,4096]{1,0:T(8,128)S(1)} %copy-done.2, f32[16,4096]{1,0:T(8,128)S(1)} %collective-permute-done.1.after_ref, f32[64,16,128]{2,1,0:T(8,128)S(1)} %bitcast.13, ...), custom_call_target="tpu_custom_call" | custom-call | tf_op jit(solution)/shard_map/near_and_sum/pallas_call | solution.py:435
  (3 shorter events, 0.0 us)
Async XLA Ops:
  0.0 54.3 %copy-start.2 = (f32[16,4096]{1,0:T(8,128)S(1)}, f32[16,4096]{1,0:T(8,128)}, u32[]{:S(2)}) copy-start(f32[16,4096]{1,0:T(8,128)} %own_ref.1) | copy-start | bytes 786436
  0.0 54.3 %collective-permute-start.1 = (f32[16,4096]{1,0:T(8,128)}, f32[16,4096]{1,0:T(8,128)S(1)}, u32[]{:S(2)}, u32[]{:S(2)}) collective-permute-start(f32[16,4096]{1,0:T(8,128)} %own_ref.1), channel_id=1, source_target_pairs={{1,0},{2,1},{3,2},{4,3},{5,4},{6,5},{7,6},{8,7},{9,8},{10,9},{11,1... | collective-permute-start | bytes 786440 | tf_op jit(solution)/shard_map/ppermute | solution.py:327
  1.4 52.9 %collective-permute-start = (f32[16,4096]{1,0:T(8,128)}, f32[16,4096]{1,0:T(8,128)S(1)}, u32[]{:S(2)}, u32[]{:S(2)}) collective-permute-start(f32[16,4096]{1,0:T(8,128)} %own_ref.1), channel_id=1, source_target_pairs={{0,1},{1,2},{2,3},{3,4},{4,5},{5,6},{6,7},{7,8},{8,9},{9,10},{10,1... | collective-permute-start | bytes 786440 | tf_op jit(solution)/shard_map/ppermute | solution.py:326
  5.6 1.0 %copy-start.1 = (f32[16,4096]{1,0:T(8,128)S(1)}, f32[16,4096]{1,0:T(8,128)}, u32[]{:S(2)}) copy-start(f32[16,4096]{1,0:T(8,128)} %own_ref.1) | copy-start | bytes 786436
  9.0 33.3 %collective-permute-start.3 = (f32[64,512]{1,0:T(8,128)S(1)}, f32[64,512]{1,0:T(8,128)S(1)}, u32[]{:S(2)}, u32[]{:S(2)}) collective-permute-start(f32[64,512]{1,0:T(8,128)S(1)} %copy.16.coef_ref.near_coef_ref), channel_id=1, source_target_pairs={{1,0},{2,1},{3,2},{4,3},{5,4},{6,5},{7,6},{8,7},{9,8},{10,9},{11,1... | collective-permute-start | bytes 393224 | tf_op jit(solution)/shard_map/ppermute | solution.py:340
  10.3 32.0 %collective-permute-start.2 = (f32[64,512]{1,0:T(8,128)S(1)}, f32[64,512]{1,0:T(8,128)S(1)}, u32[]{:S(2)}, u32[]{:S(2)}) collective-permute-start(f32[64,512]{1,0:T(8,128)S(1)} %copy.16.coef_ref.near_coef_ref), channel_id=1, source_target_pairs={{0,1},{1,2},{2,3},{3,4},{4,5},{5,6},{6,7},{7,8},{8,9},{9,10},{10,1... | collective-permute-start | bytes 393224 | tf_op jit(solution)/shard_map/ppermute | solution.py:339
  18.4 1.0 %copy-start.3 = (f32[64,1024]{1,0:T(8,128)S(1)}, f32[64,1024]{1,0:T(8,128)}, u32[]{:S(2)}) copy-start(f32[64,1024]{1,0:T(8,128)} %transfer_ref.3) | copy-start | bytes 786436
  42.4 1.6 %copy-start = (f32[64,8,1024]{2,1,0:T(8,128)S(1)}, f32[64,8,1024]{2,1,0:T(8,128)}, u32[]{:S(2)}) copy-start(f32[64,8,1024]{2,1,0:T(8,128)} %param.18) | copy-start | bytes 6291460
  44.0 0.9 %copy-start.4 = (f32[64,1024]{1,0:T(8,128)S(1)}, f32[64,1024]{1,0:T(8,128)}, u32[]{:S(2)}) copy-start(f32[64,1024]{1,0:T(8,128)} %transfer_ref.3) | copy-start | bytes 786436

commit v2 on v1

v2 whole, which is shorter than its diff:
```python
import functools

import jax
import jax.numpy as jnp
from jax import lax
from jax.experimental import pallas as pl
from jax.experimental.pallas import tpu as pltpu
from jax.sharding import PartitionSpec as P

LEAF = 64
K = 32
RHS = 16
FAR0 = 8
FAR1 = 8
NEAR = 8
LANES = 128
KR = K * RHS
KK = K * K
CHUNK = 8

f32 = jnp.float32
bf16 = jnp.bfloat16
MESH = pl.DeviceIdType.MESH
VMEM = pl.BlockSpec(memory_space=pltpu.VMEM)
SMEM = pl.BlockSpec(memory_space=pltpu.SMEM)
NT = (((1,), (1,)), ((), ()))
NN = (((1,), (0,)), ((), ()))


def halves(value):
    high = value.astype(bf16)
    low = (value - high.astype(f32)).astype(bf16)
    return high, low


def mm(a, b, dims=NN):
    return lax.dot_general(a, b, dims, preferred_element_type=f32)


def pick(value, chosen):
    high, low = halves(value)
    return mm(high, chosen) + mm(low, chosen)


def iota(shape, dim):
    return lax.broadcasted_iota(jnp.int32, shape, dim)


def mask(condition):
    return jnp.where(condition, 1.0, 0.0).astype(bf16)


def doubled_pair(pair):
    first = iota(pair.shape, 1) < LEAF
    turned = pltpu.roll(pair, LEAF, 1)
    zero = jnp.zeros_like(pair)
    even = jnp.concatenate([jnp.where(first, pair, zero), jnp.where(first, zero, turned)], axis=0)
    odd = jnp.concatenate([jnp.where(first, turned, zero), jnp.where(first, zero, pair)], axis=0)
    return even, odd


def coef_kernel(x_ref, basis_ref, coef_ref):
    def step(p, carry):
        pair = x_ref[:, pl.ds(pl.multiple_of(p * LANES, LANES), LANES)]
        for side, doubled in enumerate(doubled_pair(pair)):
            xh, xl = halves(doubled)
            bh, bl = halves(basis_ref[2 * p + side])
            both = jnp.concatenate([bh, bl], axis=1)
            twice = jnp.concatenate([xh, xh], axis=1)
            coef_ref[2 * p + side] = mm(both, twice, NT) + mm(bh, xl, NT)
        return carry

    lax.fori_loop(0, basis_ref.shape[0] // 2, step, 0, unroll=4)


def turn(src, rows, dst_ref, lane):
    here = min(LANES, src.shape[0] - rows)
    for c in range(src.shape[1] // LANES):
        block = src[rows : rows + here, c * LANES : (c + 1) * LANES]
        if here < LANES:
            block = jnp.concatenate([block, jnp.zeros((LANES - here, LANES), f32)], axis=0)
        dst_ref[c * LANES : (c + 1) * LANES, lane : lane + LANES] = block.T


def small_products(at_ref, g_ref, out_ref, tiles, transposed=False):
    width = 8

    def step(i, carry):
        tile, kb = i // (K // width), i % (K // width)
        lanes = pl.ds(pl.multiple_of(tile * LANES, LANES), LANES)
        acc = [jnp.zeros((RHS, LANES), f32)] * width
        for l8 in range(0, K, 8):
            if transposed:
                at = [at_ref[pl.ds(pl.multiple_of(kb * 8, 8) + l * K, 8), lanes] for l in range(l8, l8 + 8)]
            else:
                at = [at_ref[pl.ds(pl.multiple_of(kb * 8 * K, 8 * K) + j * K + l8, 8), lanes] for j in range(width)]
            for i in range(8):
                g = g_ref[(l8 + i) * RHS : (l8 + i + 1) * RHS, lanes]
                for j in range(width):
                    row = at[i][j : j + 1] if transposed else at[j][i : i + 1]
                    acc[j] = acc[j] + row * g
        for j in range(width):
            start = pl.multiple_of(kb * (width * RHS) + j * RHS, RHS)
            out_ref[pl.ds(start, RHS), lanes] = acc[j]
        return carry

    lax.fori_loop(0, tiles * (K // width), step, 0)


def tree_kernel(base, cpd, nleaf, ngroup,
                idx_ref, x_ref, coef_ref, transfer_ref, small_ref, leaf_idx_ref, cluster_idx_ref, near_hbm, coupling_hbm,
                near_out, field_ref,
                near_ref, coupling_ref, xb, xa, coef_ext, block_ref, gathered_ref, group_ref, sums,
                xh_ref, xl_ref, place_ref, part_ref,
                et, ct, st, lt, gt, gl, work, lwork, small_g,
                local_sem, x_sem, coef_sem, leaf_send, leaf_recv, group_send, group_recv):
    leaves = transfer_ref.shape[0]
    per = leaves // cpd
    slots = leaves * FAR0
    wide = cpd * FAR1
    g, z = lax.axis_index("group"), lax.axis_index("leaf")
    size = nleaf * ngroup
    device = g * nleaf + z
    following, preceding = lax.rem(device + 1, size), lax.rem(device + size - 1, size)
    next_id = (following // nleaf, lax.rem(following, nleaf))
    prev_id = (preceding // nleaf, lax.rem(preceding, nleaf))
    has_next, has_prev = device < size - 1, device > 0
    cross_next = has_next & (z == nleaf - 1)
    cross_prev = has_prev & (z == 0)

    near_copy = pltpu.make_async_copy(near_hbm, near_ref, local_sem.at[0])
    coupling_copy = pltpu.make_async_copy(coupling_hbm, coupling_ref, local_sem.at[1])
    coupling_copy.start()
    near_copy.start()

    barrier = pltpu.get_barrier_semaphore()

    def greet_leaf(d, carry):
        pl.semaphore_signal(barrier, inc=1, device_id=(g, lax.rem(z + d, nleaf)), device_id_type=MESH)
        return carry

    def greet_group(d, carry):
        pl.semaphore_signal(barrier, inc=1, device_id=(lax.rem(g + d, ngroup), z), device_id_type=MESH)
        return carry

    lax.fori_loop(1, nleaf, greet_leaf, 0)
    lax.fori_loop(1, ngroup, greet_group, 0)

    @pl.when(cross_next)
    def _():
        pl.semaphore_signal(barrier, inc=1, device_id=next_id, device_id_type=MESH)

    @pl.when(cross_prev)
    def _():
        pl.semaphore_signal(barrier, inc=1, device_id=prev_id, device_id_type=MESH)

    def build(ref, part):
        def step(p, carry):
            pair = ref[:, pl.ds(pl.multiple_of(p * LANES, LANES), LANES)]
            for side, doubled in enumerate(doubled_pair(pair)):
                high, low = halves(doubled)
                xh_ref[part * leaves + 2 * p + side] = high
                xl_ref[part * leaves + 2 * p + side] = low
            return carry

        lax.fori_loop(0, leaves // 2, step, 0, unroll=4)

    turn(coef_ref, 0, ct, 0)
    turn(transfer_ref, 0, et, 0)
    turn(small_ref, 0, st, 0)
    coef_ext[leaves : 2 * leaves] = coef_ref[...]

    @pl.when(jnp.logical_not(has_prev))
    def _():
        xb[...] = jnp.zeros_like(xb)
        coef_ext[0:leaves] = jnp.zeros((leaves, KR), f32)

    @pl.when(jnp.logical_not(has_next))
    def _():
        xa[...] = jnp.zeros_like(xa)
        coef_ext[2 * leaves : 3 * leaves] = jnp.zeros((leaves, KR), f32)

    enough = nleaf + ngroup - 2
    crossing = cross_next | cross_prev

    @pl.when(crossing)
    def _():
        pl.semaphore_wait(barrier, enough + 1)

    @pl.when(jnp.logical_not(crossing))
    def _():
        pl.semaphore_wait(barrier, enough)

    def to_next(src, dst, sem):
        return pltpu.make_async_remote_copy(
            src_ref=src, dst_ref=dst, send_sem=sem.at[0], recv_sem=sem.at[2], device_id=next_id, device_id_type=MESH)

    def to_prev(src, dst, sem):
        return pltpu.make_async_remote_copy(
            src_ref=src, dst_ref=dst, send_sem=sem.at[1], recv_sem=sem.at[3], device_id=prev_id, device_id_type=MESH)

    moves = (
        (x_ref, xb, xa, x_sem),
        (coef_ref, coef_ext.at[pl.ds(0, leaves)], coef_ext.at[pl.ds(2 * leaves, leaves)], coef_sem),
    )

    @pl.when(has_next)
    def _():
        for src, before, after, sem in moves:
            to_next(src, before, sem).start()

    @pl.when(has_prev)
    def _():
        for src, before, after, sem in moves:
            to_prev(src, after, sem).start()

    def finish(move):
        src, before, after, sem = move

        @pl.when(has_next)
        def _():
            to_next(src, before, sem).wait_send()
            to_prev(src, after, sem).wait_recv()

        @pl.when(has_prev)
        def _():
            to_prev(src, after, sem).wait_send()
            to_next(src, before, sem).wait_recv()

    small_products(et, ct, work, 1)
    t, q = iota((LANES, LANES), 0), iota((LANES, LANES), 1)
    chosen = mask((q - base == t // per) & (t < leaves))
    small_g[...] = pick(work[...], chosen)
    small_products(st, small_g, work, 1)
    for c in range(KR // LANES):
        rows = slice(c * LANES, (c + 1) * LANES)
        block_ref[0:8, rows] = small_g[rows, :].T[base : base + 8]
        total = jnp.sum(work[rows, :].T[base : base + cpd], axis=0, keepdims=True)
        block_ref[8:16, rows] = jnp.broadcast_to(total, (8, LANES))

    def to_leaf(d):
        return pltpu.make_async_remote_copy(
            src_ref=block_ref, dst_ref=gathered_ref.at[z], send_sem=leaf_send.at[d], recv_sem=leaf_recv.at[z],
            device_id=(g, lax.rem(z + d, nleaf)), device_id_type=MESH)

    def from_leaf(d):
        peer = lax.rem(z + d, nleaf)
        return pltpu.make_async_remote_copy(
            src_ref=block_ref, dst_ref=gathered_ref.at[peer], send_sem=leaf_send.at[d], recv_sem=leaf_recv.at[peer],
            device_id=(g, peer), device_id_type=MESH)

    def start_leaf(d, carry):
        to_leaf(d).start()
        return carry

    def wait_leaf(d, carry):
        from_leaf(d).wait()
        return carry

    def group_copy(d, outgoing):
        peer = lax.rem(g + d, ngroup)
        at = g if outgoing else peer
        return pltpu.make_async_remote_copy(
            src_ref=sums, dst_ref=group_ref.at[at], send_sem=group_send.at[d], recv_sem=group_recv.at[at],
            device_id=(peer, z), device_id_type=MESH)

    lax.fori_loop(1, nleaf, start_leaf, 0)
    gathered_ref[z] = block_ref[...]

    build(x_ref, 1)
    xh_ref[3 * leaves] = jnp.zeros(xh_ref.shape[1:], bf16)
    xl_ref[3 * leaves] = jnp.zeros(xl_ref.shape[1:], bf16)
    row, col = iota((2 * LANES, LANES), 0), iota((2 * LANES, LANES), 1)
    for side in range(2):
        for half in range(2):
            place_ref[2 * side + half] = mask(col == side * LEAF + 2 * (row // NEAR) + half)
    coupling_copy.wait()
    for tile in range(slots // LANES):
        turn(coupling_ref, tile * LANES, lt, tile * LANES)
    finish(moves[0])
    build(xb, 0)
    build(xa, 2)
    near_copy.wait()

    slot_of_lane = iota((2 * RHS, 2 * LANES), 1) % NEAR

    def near_chunk(chunk, carry):
        for i in range(CHUNK):
            n = near_ref[chunk * CHUNK + i]
            rows = jnp.concatenate([n[:, c * LANES : (c + 1) * LANES] for c in range(LEAF // 2)], axis=0)
            nh, nl = halves(rows)
            weights = jnp.concatenate([nh, nl], axis=1)
            at = [idx_ref[(chunk * CHUNK + i) * NEAR + j] for j in range(NEAR)]
            xh = jnp.concatenate([xh_ref[s] for s in at], axis=0)
            xl = jnp.concatenate([xl_ref[s] for s in at], axis=0)
            full = mm(jnp.concatenate([xh, xh], axis=1), weights, NT) + mm(
                jnp.concatenate([xl, xl], axis=1), weights, NT
            )
            kept = full[: 2 * RHS]
            for j in range(1, NEAR):
                kept = jnp.where(slot_of_lane == j, full[j * 2 * RHS : (j + 1) * 2 * RHS], kept)
            part_ref[i] = kept
        total = jnp.zeros((CHUNK // 2 * RHS, LANES), f32)
        for side in range(2):
            for half in range(2):
                rows = jnp.concatenate(
                    [part_ref[2 * p + side, half * RHS : (half + 1) * RHS] for p in range(CHUNK // 2)], axis=0
                )
                total = total + pick(rows, place_ref[2 * side + half])
        for p in range(CHUNK // 2):
            lanes = pl.ds(pl.multiple_of(chunk * (CHUNK * LEAF) + p * LANES, LANES), LANES)
            near_out[:, lanes] = total[p * RHS : (p + 1) * RHS]
        return carry

    chunks = leaves // CHUNK
    lax.fori_loop(0, chunks // 2, near_chunk, 0)

    lax.fori_loop(1, nleaf, wait_leaf, 0)

    def add(i, total):
        return total + gathered_ref[i, 8:16]

    total = lax.fori_loop(0, nleaf, add, jnp.zeros((8, KR), f32))
    sums[...] = total
    group_ref[g] = total
    for d in range(1, ngroup):
        group_copy(d, True).start()

    lax.fori_loop(chunks // 2, chunks, near_chunk, 0)

    finish(moves[1])
    for part in range(-(-3 * leaves // LANES)):
        turn(coef_ext, part * LANES, ct, part * LANES)
    onehot = mask(iota((ct.shape[1], slots), 0) == leaf_idx_ref[...])
    gl[...] = pick(ct[...], onehot)
    small_products(lt, gl, lwork, slots // LANES)

    for d in range(1, ngroup):
        group_copy(d, False).wait()
    count = gt.shape[1]
    rows = nleaf * 16
    for part in range(-(-rows // LANES)):
        first = part * LANES // 16
        here = min(LANES // 16, nleaf - first)
        turn(gathered_ref[first : first + here].reshape(here * 16, KR), 0, gt, part * LANES)
    turn(group_ref[...].reshape(ngroup * 8, KR), 0, gt, count - LANES)
    onehot = mask(iota((count, LANES), 0) == cluster_idx_ref[...])
    small_g[...] = pick(gt[...], onehot)
    small_products(st, small_g, work, 1)
    a, b = t, q
    mine = (b >= base) & (b < base + cpd)
    top = mask((a >= wide) & (a < wide + ngroup) & mine)
    small_g[...] = pick(work[...], top)
    slot = mask((a < wide) & (b - base == a // FAR1))
    far = pick(work[...], slot)
    small_products(st, small_g, work, 1, transposed=True)
    spread = mask((a - base == b // per) & (b < leaves))
    small_g[...] = pick(far + work[...], spread)
    small_products(et, small_g, work, 1, transposed=True)
    gather = mask(iota((slots, LANES), 0) // FAR0 == iota((slots, LANES), 1))
    field = work[...] + pick(lwork[...], gather)
    for c in range(KR // LANES):
        rows_c = slice(c * LANES, (c + 1) * LANES)
        field_ref[:, rows_c] = field[rows_c].T[:leaves]


def sum_kernel(near_ref, basis_ref, field_ref, out_ref):
    first = iota((RHS, LANES), 1) < LEAF

    def step(p, carry):
        ends = []
        for side in range(2):
            i = 2 * p + side
            fh, fl = halves(field_ref[i])
            bh, bl = halves(basis_ref[i])
            wide = mm(jnp.concatenate([fh, fl], axis=0), jnp.concatenate([bh, bl], axis=1))
            both = wide[: 2 * RHS, :LANES] + wide[: 2 * RHS, LANES:] + wide[2 * RHS :, :LANES]
            ends.append((both[:RHS], both[RHS:]))
        straight = jnp.where(first, ends[0][0], ends[1][1])
        crossed = jnp.where(first, ends[1][0], ends[0][1])
        lanes = pl.ds(pl.multiple_of(p * LANES, LANES), LANES)
        out_ref[:, lanes] = near_ref[:, lanes] + straight + pltpu.roll(crossed, LEAF, 1)
        return carry

    lax.fori_loop(0, basis_ref.shape[0] // 2, step, 0, unroll=4)


def params(**kw):
    return pltpu.CompilerParams(vmem_limit_bytes=48 * 1024 * 1024, **kw)


def per_device(
    right_sides,
    near_blocks,
    near_source,
    near_count,
    basis,
    leaf_source,
    leaf_coupling,
    leaf_transfer,
    cluster_source,
    cluster_coupling,
    cluster_transfer,
    group_coupling,
):
    leaves = near_blocks.shape[0]
    cpd = cluster_coupling.shape[0]
    ngroup, nleaf = lax.axis_size("group"), lax.axis_size("leaf")
    device = lax.axis_index(("group", "leaf"))
    window_start = (device - 1) * leaves
    basis3 = basis.reshape(leaves, K * LEAF // LANES, LANES)
    coef = pl.pallas_call(
        coef_kernel,
        out_shape=jax.ShapeDtypeStruct((leaves, K // 2, 2 * RHS), f32),
        in_specs=[VMEM, VMEM],
        out_specs=VMEM,
        compiler_params=params(),
        name="leaf_coefficients",
    )(right_sides, basis3)
    coef = coef.reshape(leaves, KR)
    wide = cpd * FAR1
    base = wide + 8
    assert ngroup <= 8 and cpd <= 8 and base + 8 <= LANES and leaves <= LANES
    small = jnp.concatenate(
        [
            cluster_coupling.reshape(wide, KK),
            jnp.pad(group_coupling.reshape(ngroup, KK), ((0, 8 - ngroup), (0, 0))),
            jnp.pad(cluster_transfer, ((0, 8 - cpd), (0, 0))),
        ],
        axis=0,
    )
    rows = nleaf * 16
    padded = -(-rows // LANES) * LANES
    source_row = cluster_source // cpd * 16 + cluster_source % cpd
    cluster_idx = jnp.concatenate(
        [
            source_row.reshape(1, wide),
            padded + 8 * jnp.arange(ngroup, dtype=jnp.int32).reshape(1, ngroup),
            jnp.full((1, LANES - wide - ngroup), -1, jnp.int32),
        ],
        axis=1,
    )
    leaf_idx = (leaf_source - window_start).reshape(1, leaves * FAR0)
    source_lanes = -(-3 * leaves // LANES) * LANES
    slots = leaves * FAR0
    live = jnp.arange(NEAR, dtype=jnp.int32)[None, :] < near_count[:, None]
    near_idx = jnp.where(live, near_source - window_start, 3 * leaves).reshape(leaves * NEAR)
    near, field = pl.pallas_call(
        functools.partial(tree_kernel, base, cpd, nleaf, ngroup),
        out_shape=(
            jax.ShapeDtypeStruct((RHS, leaves * LEAF), f32),
            jax.ShapeDtypeStruct((leaves, KR), f32),
        ),
        in_specs=[SMEM] + [VMEM] * 6 + [pl.BlockSpec(memory_space=pl.ANY)] * 2,
        out_specs=(VMEM, VMEM),
        scratch_shapes=[
            pltpu.VMEM((leaves, NEAR, LEAF * LEAF), f32),
            pltpu.VMEM((slots, KK), f32),
            pltpu.VMEM((RHS, leaves * LEAF), f32),
            pltpu.VMEM((RHS, leaves * LEAF), f32),
            pltpu.VMEM((3 * leaves, KR), f32),
            pltpu.VMEM((16, KR), f32),
            pltpu.VMEM((nleaf, 16, KR), f32),
            pltpu.VMEM((ngroup, 8, KR), f32),
            pltpu.VMEM((8, KR), f32),
            pltpu.VMEM((3 * leaves + 1, 2 * RHS, LANES), bf16),
            pltpu.VMEM((3 * leaves + 1, 2 * RHS, LANES), bf16),
            pltpu.VMEM((4, 2 * LANES, LANES), bf16),
            pltpu.VMEM((CHUNK, 2 * RHS, 2 * LANES), f32),
            pltpu.VMEM((KK, LANES), f32),
            pltpu.VMEM((KR, source_lanes), f32),
            pltpu.VMEM((KK, LANES), f32),
            pltpu.VMEM((KK, slots), f32),
            pltpu.VMEM((KR, padded + LANES), f32),
            pltpu.VMEM((KR, slots), f32),
            pltpu.VMEM((KR, LANES), f32),
            pltpu.VMEM((KR, slots), f32),
            pltpu.VMEM((KR, LANES), f32),
            pltpu.SemaphoreType.DMA((2,)),
            pltpu.SemaphoreType.DMA((4,)),
            pltpu.SemaphoreType.DMA((4,)),
            pltpu.SemaphoreType.DMA((nleaf,)),
            pltpu.SemaphoreType.DMA((nleaf,)),
            pltpu.SemaphoreType.DMA((ngroup,)),
            pltpu.SemaphoreType.DMA((ngroup,)),
        ],
        compiler_params=params(collective_id=0, has_side_effects=True),
        name="tree_and_near",
    )(
        near_idx,
        right_sides,
        coef,
        leaf_transfer,
        small,
        leaf_idx,
        cluster_idx,
        near_blocks,
        leaf_coupling.reshape(slots, KK),
    )
    field = field.reshape(leaves, K // 2, 2 * RHS).transpose(0, 2, 1)
    return pl.pallas_call(
        sum_kernel,
        out_shape=jax.ShapeDtypeStruct((RHS, leaves * LEAF), f32),
        in_specs=[VMEM] * 3,
        out_specs=VMEM,
        compiler_params=params(),
        name="sum",
    )(near, basis3, field)


def solution(mesh):
    split = P(("group", "leaf"))
    in_specs = (
        P(None, ("group", "leaf")),
        split,
        split,
        split,
        split,
        split,
        split,
        split,
        split,
        split,
        split,
        P("group"),
    )
    return jax.shard_map(
        per_device, mesh=mesh, in_specs=in_specs, out_specs=P(None, ("group", "leaf")), check_vma=False
    )
```

time: 68.1 us -> 48.9 us (0.72)
  starting transfers between devices: 10.9 us -> 0 us
  Pallas kernels: 46.4 us -> 38.5 us
    ppermute x4 -> x0, starting transfers between devices: 10.9 us -> none  [the longest x1 5.17 us: per_device(): coef_before = lax.ppermute(coef, axes, up)]
    pallas_call x4 -> x2, Pallas kernels: 44.4 us -> 36.4 us  [the longest x1 33.5 us: per_device(): pl.pallas_call(functools.partial(tree_kernel, base, cpd, nleaf, ngroup),...]
    unnamed x11 -> x9, local copies, waits for them, and re-layouts: 5.57 us -> 5.57 us
  transfers between devices with their start and end apart: 4 -> 0, of which waited for: 0 -> 0; matrix products, arithmetic and copies ran while one was open for 8% -> 0% of each run, Pallas kernels for 49% -> 0%
where the time goes in v2:
time: 48.9 us; the launch traced here: 48.5 us
  Pallas kernels  38.5 us (79%)
  local copies, waits for them, and re-layouts  7.46 us (15%)
  other arithmetic  2.46 us (5%)
    pallas_call x1, Pallas kernels, per_device(): pl.pallas_call(functools.partial(tree_kernel, base, cpd, nleaf, ngroup),...  33.5 us
    unnamed x9, local copies, waits for them, and re-layouts  5.57 us
    pallas_call x1, Pallas kernels, per_device(): pl.pallas_call(sum_kernel, out_shape=jax.ShapeDtypeStruct((RHS, leaves *...  2.91 us
    pallas_call x1, Pallas kernels, per_device(): pl.pallas_call(coef_kernel, out_shape=jax.ShapeDtypeStruct((leaves, K //...  2.08 us

profile of v2, /device:TPU:0, one launch (start us, length us, event | category | flops | bytes accessed | tf_op | source)
XLA Modules:
  0.0 48.5 jit_solution(4241021202292118089)
XLA Ops:
  0.0 0.7 %fusion.2 = s32[4,8]{1,0:T(4,128)S(1)} fusion(s32[4,8]{1,0:T(4,128)} %param.20), kind=kLoop, calls=%fused_computation.14 | loop fusion | flops 672 | bytes 256 | tf_op jit(solution)/shard_map/add | solution.py:434
  0.7 0.1 reshape.47
  0.8 0.1 bitcast_add_fusion.cluster_idx_ref
  0.9 0.7 %subtract_select_fusion = (s32[64,8]{0,1:T(8,128)S(1)}, s32[64,8]{0,1:T(8,128)S(1)}) fusion(s32[64,8]{0,1:T(8,128)} %param.14, s32[]{:T(128)S(6)} %mul.24, s32[64]{0:T(128)} %param.15, s32[64,8]{0,1:T(8,128)} %param.17), kind=kLoop, calls=%fused_computation.6 | loop fusion | flops 2048 | bytes 8452 | tf_op jit(solution)/shard_map/jit(_where)/select_n | solution.py:447
  1.6 0.1 copy.14
  1.7 0.1 reshape.41.idx_ref
  1.8 0.1 copy.16
  1.9 0.1 reshape.46.leaf_idx_ref
  1.9 1.0 %select_maximum_fusion.small_ref = f32[48,1024]{1,0:T(8,128)S(1)} fusion(f32[4,1024]{1,0:T(4,128)} %param.22, f32[4,1024]{1,0:T(4,128)} %bitcast.18, f32[32,1024]{1,0:T(8,128)} %bitcast.17), kind=kLoop, calls=%fused_computation.2 | loop fusion | flops 393216 | bytes 360448 | tf_op jit(solution)/shard_map/concatenate | solution.py:424
  2.9 1.1 %copy.20 = f32[8,8,16,128]{3,2,1,0:T(8,128)S(1)} copy(f32[8,8,16,128]{3,1,2,0:T(8,128)} %bitcast.16) | data formatting | bytes 1048576
  4.0 0.0 copy-start.1
  4.1 0.9 %copy-done.1 = f32[16,4096]{1,0:T(8,128)S(1)} copy-done((f32[16,4096]{1,0:T(8,128)S(1)}, f32[16,4096]{1,0:T(8,128)}, u32[]{:S(2)}) %copy-start.1) | copy-done | bytes 262168
  5.0 2.1 %leaf_coefficients.1 = f32[64,16,32]{2,1,0:T(8,128)S(1)} custom-call(f32[16,4096]{1,0:T(8,128)S(1)} %copy-done.1, f32[64,16,128]{2,1,0:T(8,128)S(1)} %bitcast.10), custom_call_target="tpu_custom_call" | custom-call | tf_op jit(solution)/shard_map/leaf_coefficients/pallas_call | solution.py:412
  7.1 0.3 copy.15
  7.3 0.1 copy.17.coef_ref
  7.5 0.0 copy-start
  7.5 1.6 %copy-done = f32[64,8,1024]{2,1,0:T(8,128)S(1)} copy-done((f32[64,8,1024]{2,1,0:T(8,128)S(1)}, f32[64,8,1024]{2,1,0:T(8,128)}, u32[]{:S(2)}) %copy-start) | copy-done | bytes 2097176
  9.1 0.0 copy-start.2
  9.1 0.9 %copy-done.2 = f32[16,4096]{1,0:T(8,128)S(1)} copy-done((f32[16,4096]{1,0:T(8,128)S(1)}, f32[16,4096]{1,0:T(8,128)}, u32[]{:S(2)}) %copy-start.2) | copy-done | bytes 262168
  10.0 0.0 copy-start.3
  10.0 0.9 %copy-done.3 = f32[64,1024]{1,0:T(8,128)S(1)} copy-done((f32[64,1024]{1,0:T(8,128)S(1)}, f32[64,1024]{1,0:T(8,128)}, u32[]{:S(2)}) %copy-start.3) | copy-done | bytes 262168
  11.0 33.5 %tree_and_near.1 = (f32[16,4096]{1,0:T(8,128)S(1)}, f32[64,512]{1,0:T(8,128)S(1)}) custom-call(s32[512]{0:T(512)S(1)} %reshape.41.idx_ref, f32[16,4096]{1,0:T(8,128)S(1)} %copy-done.2, f32[64,512]{1,0:T(8,128)S(1)} %copy.17.coef_ref, f32[64,1024]{1,0:T(8,128)S(1)} %copy-done.3, f32[48,1024]{1,0:T(8,128)S(1)} %select_maximum_fusion.small_ref, ...), custom_call_target="tpu_custom_call" | custom-call | tf_op jit(solution)/shard_map/tree_and_near/pallas_call | solution.py:448
  44.5 0.1 copy.18
  44.6 1.0 %copy.19 = f32[64,16,32]{1,2,0:T(8,128)S(1)} copy(f32[64,16,32]{0,2,1:T(8,128)S(1)} %bitcast.15) | data formatting | bytes 262144 | tf_op jit(solution)/shard_map/reshape | solution.py:500
  45.6 2.9 %sum.1 = f32[16,4096]{1,0:T(8,128)} custom-call(f32[16,4096]{1,0:T(8,128)S(1)} %get-tuple-element.7.near_ref, f32[64,16,128]{2,1,0:T(8,128)S(1)} %bitcast.11, f32[64,32,16]{2,1,0:T(8,128)S(1)} %bitcast.12), custom_call_target="tpu_custom_call" | custom-call | tf_op jit(solution)/shard_map/sum/pallas_call | solution.py:501
  (2 shorter events, 0.0 us)
Async XLA Ops:
  4.0 1.0 %copy-start.1 = (f32[16,4096]{1,0:T(8,128)S(1)}, f32[16,4096]{1,0:T(8,128)}, u32[]{:S(2)}) copy-start(f32[16,4096]{1,0:T(8,128)} %x_ref.3) | copy-start | bytes 786436
  7.5 1.6 %copy-start = (f32[64,8,1024]{2,1,0:T(8,128)S(1)}, f32[64,8,1024]{2,1,0:T(8,128)}, u32[]{:S(2)}) copy-start(f32[64,8,1024]{2,1,0:T(8,128)} %param.18) | copy-start | bytes 6291460
  9.1 0.9 %copy-start.2 = (f32[16,4096]{1,0:T(8,128)S(1)}, f32[16,4096]{1,0:T(8,128)}, u32[]{:S(2)}) copy-start(f32[16,4096]{1,0:T(8,128)} %x_ref.3) | copy-start | bytes 786436
  10.0 0.9 %copy-start.3 = (f32[64,1024]{1,0:T(8,128)S(1)}, f32[64,1024]{1,0:T(8,128)}, u32[]{:S(2)}) copy-start(f32[64,1024]{1,0:T(8,128)} %transfer_ref.1) | copy-start | bytes 786436

commit v3 on v2

--- a/solution.py
+++ b/solution.py
@@ -25,6 +25,7 @@
 SMEM = pl.BlockSpec(memory_space=pltpu.SMEM)
 NT = (((1,), (1,)), ((), ()))
 NN = (((1,), (0,)), ((), ()))
+TN = (((0,), (0,)), ((), ()))
 
 
 def halves(value):
@@ -70,7 +71,7 @@
             coef_ref[2 * p + side] = mm(both, twice, NT) + mm(bh, xl, NT)
         return carry
 
-    lax.fori_loop(0, basis_ref.shape[0] // 2, step, 0, unroll=4)
+    lax.fori_loop(0, basis_ref.shape[0] // 2, step, 0, unroll=8)
 
 
 def turn(src, rows, dst_ref, lane):
@@ -108,9 +109,11 @@
 
 
 def tree_kernel(base, cpd, nleaf, ngroup,
-                idx_ref, x_ref, coef_ref, transfer_ref, small_ref, leaf_idx_ref, cluster_idx_ref, near_hbm, coupling_hbm,
+                source_ref, count_ref, coef_ref, leaf_source_ref, cluster_source_ref,
+                cluster_coupling_ref, group_coupling_ref, cluster_transfer_ref,
+                x_hbm, transfer_hbm, near_hbm, coupling_hbm,
                 near_out, field_ref,
-                near_ref, coupling_ref, xb, xa, coef_ext, block_ref, gathered_ref, group_ref, sums,
+                x_ref, transfer_ref, small_ref, near_ref, coupling_ref, xb, xa, coef_ext, block_ref, gathered_ref, group_ref, sums,
                 xh_ref, xl_ref, place_ref, part_ref,
                 et, ct, st, lt, gt, gl, work, lwork, small_g,
                 local_sem, x_sem, coef_sem, leaf_send, leaf_recv, group_send, group_recv):
@@ -130,6 +133,10 @@
 
     near_copy = pltpu.make_async_copy(near_hbm, near_ref, local_sem.at[0])
     coupling_copy = pltpu.make_async_copy(coupling_hbm, coupling_ref, local_sem.at[1])
+    x_copy = pltpu.make_async_copy(x_hbm, x_ref, local_sem.at[2])
+    transfer_copy = pltpu.make_async_copy(transfer_hbm, transfer_ref, local_sem.at[3])
+    transfer_copy.start()
+    x_copy.start()
     coupling_copy.start()
     near_copy.start()
 
@@ -163,11 +170,16 @@
                 xl_ref[part * leaves + 2 * p + side] = low
             return carry
 
-        lax.fori_loop(0, leaves // 2, step, 0, unroll=4)
+        lax.fori_loop(0, leaves // 2, step, 0, unroll=8)
 
     turn(coef_ref, 0, ct, 0)
+    small_ref[...] = jnp.zeros_like(small_ref)
+    small_ref[0:wide] = cluster_coupling_ref[...]
+    small_ref[wide : wide + ngroup] = group_coupling_ref[...]
+    small_ref[base : base + cpd] = cluster_transfer_ref[...]
+    turn(small_ref, 0, st, 0)
+    transfer_copy.wait()
     turn(transfer_ref, 0, et, 0)
-    turn(small_ref, 0, st, 0)
     coef_ext[leaves : 2 * leaves] = coef_ref[...]
 
     @pl.when(jnp.logical_not(has_prev))
@@ -200,7 +212,7 @@
             src_ref=src, dst_ref=dst, send_sem=sem.at[1], recv_sem=sem.at[3], device_id=prev_id, device_id_type=MESH)
 
     moves = (
-        (x_ref, xb, xa, x_sem),
+        (x_hbm, xb, xa, x_sem),
         (coef_ref, coef_ext.at[pl.ds(0, leaves)], coef_ext.at[pl.ds(2 * leaves, leaves)], coef_sem),
     )
 
@@ -267,6 +279,7 @@
     lax.fori_loop(1, nleaf, start_leaf, 0)
     gathered_ref[z] = block_ref[...]
 
+    x_copy.wait()
     build(x_ref, 1)
     xh_ref[3 * leaves] = jnp.zeros(xh_ref.shape[1:], bf16)
     xl_ref[3 * leaves] = jnp.zeros(xl_ref.shape[1:], bf16)
@@ -290,7 +303,11 @@
             rows = jnp.concatenate([n[:, c * LANES : (c + 1) * LANES] for c in range(LEAF // 2)], axis=0)
             nh, nl = halves(rows)
             weights = jnp.concatenate([nh, nl], axis=1)
-            at = [idx_ref[(chunk * CHUNK + i) * NEAR + j] for j in range(NEAR)]
+            leaf = chunk * CHUNK + i
+            live = count_ref[leaf]
+            at = [
+                jnp.where(j < live, source_ref[j, leaf] - (device - 1) * leaves, 3 * leaves) for j in range(NEAR)
+            ]
             xh = jnp.concatenate([xh_ref[s] for s in at], axis=0)
             xl = jnp.concatenate([xl_ref[s] for s in at], axis=0)
             full = mm(jnp.concatenate([xh, xh], axis=1), weights, NT) + mm(
@@ -331,7 +348,12 @@
     finish(moves[1])
     for part in range(-(-3 * leaves // LANES)):
         turn(coef_ext, part * LANES, ct, part * LANES)
-    onehot = mask(iota((ct.shape[1], slots), 0) == leaf_idx_ref[...])
+    local = (leaf_source_ref[...] - (device - 1) * leaves).astype(f32)
+    lane = iota((leaves, slots), 1)
+    expanded = mm(local.astype(bf16), mask(lane // FAR0 == iota((leaves, slots), 0)))
+    lane = iota((FAR0, slots), 1)
+    wanted = jnp.sum(jnp.where(lane % FAR0 == iota((FAR0, slots), 0), expanded, 0.0), axis=0, keepdims=True)
+    onehot = mask(iota((ct.shape[1], slots), 0) == wanted.astype(jnp.int32))
     gl[...] = pick(ct[...], onehot)
     small_products(lt, gl, lwork, slots // LANES)
 
@@ -344,7 +366,15 @@
         here = min(LANES // 16, nleaf - first)
         turn(gathered_ref[first : first + here].reshape(here * 16, KR), 0, gt, part * LANES)
     turn(group_ref[...].reshape(ngroup * 8, KR), 0, gt, count - LANES)
-    onehot = mask(iota((count, LANES), 0) == cluster_idx_ref[...])
+    sources = cluster_source_ref[...]
+    lane = iota((1, LANES), 1)
+    wanted = jnp.full((1, LANES), -1, jnp.int32)
+    for u in range(cpd):
+        for j in range(FAR1):
+            wanted = jnp.where(lane == u * FAR1 + j, sources[u : u + 1, j : j + 1], wanted)
+    wanted = jnp.where(wanted >= 0, wanted // cpd * 16 + wanted % cpd, -1)
+    wanted = jnp.where((lane >= wide) & (lane < wide + ngroup), count - LANES + 8 * (lane - wide), wanted)
+    onehot = mask(iota((count, LANES), 0) == wanted)
     small_g[...] = pick(gt[...], onehot)
     small_products(st, small_g, work, 1)
     a, b = t, q
@@ -373,7 +403,7 @@
             i = 2 * p + side
             fh, fl = halves(field_ref[i])
             bh, bl = halves(basis_ref[i])
-            wide = mm(jnp.concatenate([fh, fl], axis=0), jnp.concatenate([bh, bl], axis=1))
+            wide = mm(jnp.concatenate([fh, fl], axis=1), jnp.concatenate([bh, bl], axis=1), TN)
             both = wide[: 2 * RHS, :LANES] + wide[: 2 * RHS, LANES:] + wide[2 * RHS :, :LANES]
             ends.append((both[:RHS], both[RHS:]))
         straight = jnp.where(first, ends[0][0], ends[1][1])
@@ -382,11 +412,11 @@
         out_ref[:, lanes] = near_ref[:, lanes] + straight + pltpu.roll(crossed, LEAF, 1)
         return carry
 
-    lax.fori_loop(0, basis_ref.shape[0] // 2, step, 0, unroll=4)
-
-
-def params(**kw):
-    return pltpu.CompilerParams(vmem_limit_bytes=48 * 1024 * 1024, **kw)
+    lax.fori_loop(0, basis_ref.shape[0] // 2, step, 0, unroll=8)
+
+
+def params(mib=48, **kw):
+    return pltpu.CompilerParams(vmem_limit_bytes=mib * 1024 * 1024, **kw)
 
 
 def per_device(
@@ -406,8 +436,6 @@
     leaves = near_blocks.shape[0]
     cpd = cluster_coupling.shape[0]
     ngroup, nleaf = lax.axis_size("group"), lax.axis_size("leaf")
-    device = lax.axis_index(("group", "leaf"))
-    window_start = (device - 1) * leaves
     basis3 = basis.reshape(leaves, K * LEAF // LANES, LANES)
     coef = pl.pallas_call(
         coef_kernel,
@@ -421,39 +449,22 @@
     wide = cpd * FAR1
     base = wide + 8
     assert ngroup <= 8 and cpd <= 8 and base + 8 <= LANES and leaves <= LANES
-    small = jnp.concatenate(
-        [
-            cluster_coupling.reshape(wide, KK),
-            jnp.pad(group_coupling.reshape(ngroup, KK), ((0, 8 - ngroup), (0, 0))),
-            jnp.pad(cluster_transfer, ((0, 8 - cpd), (0, 0))),
-        ],
-        axis=0,
-    )
     rows = nleaf * 16
     padded = -(-rows // LANES) * LANES
-    source_row = cluster_source // cpd * 16 + cluster_source % cpd
-    cluster_idx = jnp.concatenate(
-        [
-            source_row.reshape(1, wide),
-            padded + 8 * jnp.arange(ngroup, dtype=jnp.int32).reshape(1, ngroup),
-            jnp.full((1, LANES - wide - ngroup), -1, jnp.int32),
-        ],
-        axis=1,
-    )
-    leaf_idx = (leaf_source - window_start).reshape(1, leaves * FAR0)
     source_lanes = -(-3 * leaves // LANES) * LANES
     slots = leaves * FAR0
-    live = jnp.arange(NEAR, dtype=jnp.int32)[None, :] < near_count[:, None]
-    near_idx = jnp.where(live, near_source - window_start, 3 * leaves).reshape(leaves * NEAR)
     near, field = pl.pallas_call(
         functools.partial(tree_kernel, base, cpd, nleaf, ngroup),
         out_shape=(
             jax.ShapeDtypeStruct((RHS, leaves * LEAF), f32),
             jax.ShapeDtypeStruct((leaves, KR), f32),
         ),
-        in_specs=[SMEM] + [VMEM] * 6 + [pl.BlockSpec(memory_space=pl.ANY)] * 2,
+        in_specs=[SMEM] * 2 + [VMEM] * 6 + [pl.BlockSpec(memory_space=pl.ANY)] * 4,
         out_specs=(VMEM, VMEM),
         scratch_shapes=[
+            pltpu.VMEM((RHS, leaves * LEAF), f32),
+            pltpu.VMEM((leaves, KK), f32),
+            pltpu.VMEM((base + 8, KK), f32),
             pltpu.VMEM((leaves, NEAR, LEAF * LEAF), f32),
             pltpu.VMEM((slots, KK), f32),
             pltpu.VMEM((RHS, leaves * LEAF), f32),
@@ -476,7 +487,7 @@
             pltpu.VMEM((KR, LANES), f32),
             pltpu.VMEM((KR, slots), f32),
             pltpu.VMEM((KR, LANES), f32),
-            pltpu.SemaphoreType.DMA((2,)),
+            pltpu.SemaphoreType.DMA((4,)),
             pltpu.SemaphoreType.DMA((4,)),
             pltpu.SemaphoreType.DMA((4,)),
             pltpu.SemaphoreType.DMA((nleaf,)),
@@ -484,20 +495,23 @@
             pltpu.SemaphoreType.DMA((ngroup,)),
             pltpu.SemaphoreType.DMA((ngroup,)),
         ],
-        compiler_params=params(collective_id=0, has_side_effects=True),
+        compiler_params=params(63, collective_id=0, has_side_effects=True),
         name="tree_and_near",
     )(
-        near_idx,
+        near_source.T,
+        near_count,
+        coef,
+        leaf_source.T,
+        cluster_source,
+        cluster_coupling.reshape(wide, KK),
+        group_coupling.reshape(ngroup, KK),
+        cluster_transfer,
         right_sides,
-        coef,
         leaf_transfer,
-        small,
-        leaf_idx,
-        cluster_idx,
         near_blocks,
         leaf_coupling.reshape(slots, KK),
     )
-    field = field.reshape(leaves, K // 2, 2 * RHS).transpose(0, 2, 1)
+    field = field.reshape(leaves, K // 2, 2 * RHS)
     return pl.pallas_call(
         sum_kernel,
         out_shape=jax.ShapeDtypeStruct((RHS, leaves * LEAF), f32),

time: 48.9 us -> 44.8 us (0.916)
  other arithmetic: 2.46 us -> 0 us
  local copies, waits for them, and re-layouts: 7.46 us -> 5.38 us
  Pallas kernels: 38.5 us -> 39.1 us
    unnamed x9 -> x5, local copies, waits for them, and re-layouts: 5.57 us -> 3.02 us
    pallas_call x1, Pallas kernels: 33.5 us -> 35 us  [per_device(): pl.pallas_call(functools.partial(tree_kernel, base, cpd, nleaf, ngroup),...]
    concatenate x2 -> x0, other arithmetic: 1.04 us -> none  [the longest x1 0.96 us: per_device(): jnp.concatenate([cluster_coupling.reshape(wide, KK), jnp.pad(group_coupli...]
    reshape x4 -> x1, local copies, waits for them, and re-layouts: 1.22 us -> 0.29 us  [per_device(): field = field.reshape(leaves, K // 2, 2 * RHS)]
    pallas_call x1, local copies, waits for them, and re-layouts: 0.12 us -> 1.03 us  [per_device(): pl.pallas_call(functools.partial(tree_kernel, base, cpd, nleaf, ngroup),...]
    pallas_call x1, Pallas kernels: 2.08 us -> 1.29 us  [per_device(): pl.pallas_call(coef_kernel, out_shape=jax.ShapeDtypeStruct((leaves, K //...]
    select_n x1 -> x0, other arithmetic: 0.73 us -> none  [per_device(): jnp.where(live, near_source - window_start, 3 * leaves)]
    add x2 -> x0, other arithmetic: 0.7 us -> none  [the longest x1 0.69 us: per_device(): source_row = cluster_source // cpd * 16 + cluster_source % cpd]
where the time goes in v3:
time: 44.8 us; the launch traced here: 44.5 us
  Pallas kernels  39.1 us (87%)
  local copies, waits for them, and re-layouts  5.38 us (12%)
    pallas_call x1, Pallas kernels, per_device(): pl.pallas_call(functools.partial(tree_kernel, base, cpd, nleaf, ngroup),...  35 us
    unnamed x5, local copies, waits for them, and re-layouts  3.02 us
    pallas_call x1, Pallas kernels, per_device(): pl.pallas_call(sum_kernel, out_shape=jax.ShapeDtypeStruct((RHS, leaves *...  2.84 us
    pallas_call x1, Pallas kernels, per_device(): pl.pallas_call(coef_kernel, out_shape=jax.ShapeDtypeStruct((leaves, K //...  1.29 us
    pallas_call x1, local copies, waits for them, and re-layouts, per_device(): pl.pallas_call(functools.partial(tree_kernel, base, cpd, nleaf, ngroup),...  1.03 us

profile of v3, /device:TPU:0, one launch (start us, length us, event | category | flops | bytes accessed | tf_op | source)
XLA Modules:
  0.0 44.5 jit_solution(4299375996485166212)
XLA Ops:
  0.0 1.1 %copy.17 = f32[8,8,16,128]{3,2,1,0:T(8,128)S(1)} copy(f32[8,8,16,128]{3,1,2,0:T(8,128)} %bitcast.14) | data formatting | bytes 1048576
  1.1 0.0 copy-start
  1.2 0.9 %copy-done = f32[16,4096]{1,0:T(8,128)S(1)} copy-done((f32[16,4096]{1,0:T(8,128)S(1)}, f32[16,4096]{1,0:T(8,128)}, u32[]{:S(2)}) %copy-start) | copy-done | bytes 262168
  2.1 1.3 %leaf_coefficients.1 = f32[64,16,32]{2,1,0:T(8,128)S(1)} custom-call(f32[16,4096]{1,0:T(8,128)S(1)} %copy-done, f32[64,16,128]{2,1,0:T(8,128)S(1)} %bitcast.9), custom_call_target="tpu_custom_call" | custom-call | tf_op jit(solution)/shard_map/leaf_coefficients/pallas_call | solution.py:440
  3.4 0.3 copy.13
  3.7 0.8 %copy.14.coef_ref = f32[64,512]{1,0:T(8,128)} copy(f32[64,512]{0,1:T(8,128)S(1)} %bitcast.12) | data formatting | bytes 262144 | tf_op jit(solution)/shard_map/reshape | solution.py:448
  4.4 35.0 %tree_and_near.1 = (f32[16,4096]{1,0:T(8,128)}, f32[64,512]{1,0:T(8,128)}) custom-call(s32[8,64]{1,0:T(8,128)} %bitcast.17, s32[64]{0:T(128)} %count_ref.1, f32[64,512]{1,0:T(8,128)} %copy.14.coef_ref, s32[8,64]{1,0:T(8,128)} %bitcast.18, s32[4,8]{1,0:T(4,128)} %cluster_source_ref.1, f32[32,1024]{1,0:T(8,128)} %bitcast.15, f32[4,1024]{1,0:T(4,128)} %bitcast.16, ...), custom_call_target="tpu_custom_call" | custom-call | tf_op jit(solution)/shard_map/tree_and_near/pallas_call | solution.py:456
  39.4 1.0 %copy.15 = f32[64,512]{0,1:T(8,128)S(1)} copy(f32[64,512]{1,0:T(8,128)} %get-tuple-element.8) | data formatting | bytes 262144 | tf_op jit(solution)/shard_map/tree_and_near/pallas_call | solution.py:456
  40.4 0.3 copy.16.field_ref
  40.7 0.0 copy-start.1
  40.7 0.9 %copy-done.1 = f32[16,4096]{1,0:T(8,128)S(1)} copy-done((f32[16,4096]{1,0:T(8,128)S(1)}, f32[16,4096]{1,0:T(8,128)}, u32[]{:S(2)}) %copy-start.1) | copy-done | bytes 262168
  41.7 2.8 %sum.1 = f32[16,4096]{1,0:T(8,128)} custom-call(f32[16,4096]{1,0:T(8,128)S(1)} %copy-done.1, f32[64,16,128]{2,1,0:T(8,128)S(1)} %bitcast.10, f32[64,16,32]{2,1,0:T(8,128)S(1)} %copy.16.field_ref), custom_call_target="tpu_custom_call" | custom-call | tf_op jit(solution)/shard_map/sum/pallas_call | solution.py:515
Async XLA Ops:
  1.1 1.0 %copy-start = (f32[16,4096]{1,0:T(8,128)S(1)}, f32[16,4096]{1,0:T(8,128)}, u32[]{:S(2)}) copy-start(f32[16,4096]{1,0:T(8,128)} %x_hbm.1) | copy-start | bytes 786436
  40.7 1.0 %copy-start.1 = (f32[16,4096]{1,0:T(8,128)S(1)}, f32[16,4096]{1,0:T(8,128)}, u32[]{:S(2)}) copy-start(f32[16,4096]{1,0:T(8,128)} %get-tuple-element.7.near_ref) | copy-start | bytes 786436

commit v4 on v3

--- a/solution.py
+++ b/solution.py
@@ -109,11 +109,11 @@
 
 
 def tree_kernel(base, cpd, nleaf, ngroup,
-                source_ref, count_ref, coef_ref, leaf_source_ref, cluster_source_ref,
+                source_ref, count_ref, basis_in_ref, leaf_source_ref, cluster_source_ref,
                 cluster_coupling_ref, group_coupling_ref, cluster_transfer_ref,
                 x_hbm, transfer_hbm, near_hbm, coupling_hbm,
-                near_out, field_ref,
-                x_ref, transfer_ref, small_ref, near_ref, coupling_ref, xb, xa, coef_ext, block_ref, gathered_ref, group_ref, sums,
+                near_out, field_ref, basis_ref,
+                coef_blocks, coef_ref, x_ref, transfer_ref, small_ref, near_ref, coupling_ref, xb, xa, coef_ext, block_ref, gathered_ref, group_ref, sums,
                 xh_ref, xl_ref, place_ref, part_ref,
                 et, ct, st, lt, gt, gl, work, lwork, small_g,
                 local_sem, x_sem, coef_sem, leaf_send, leaf_recv, group_send, group_recv):
@@ -135,8 +135,8 @@
     coupling_copy = pltpu.make_async_copy(coupling_hbm, coupling_ref, local_sem.at[1])
     x_copy = pltpu.make_async_copy(x_hbm, x_ref, local_sem.at[2])
     transfer_copy = pltpu.make_async_copy(transfer_hbm, transfer_ref, local_sem.at[3])
+    x_copy.start()
     transfer_copy.start()
-    x_copy.start()
     coupling_copy.start()
     near_copy.start()
 
@@ -172,7 +172,80 @@
 
         lax.fori_loop(0, leaves // 2, step, 0, unroll=8)
 
-    turn(coef_ref, 0, ct, 0)
+
+    @pl.when(jnp.logical_not(has_prev))
+    def _():
+        xb[...] = jnp.zeros_like(xb)
+        coef_ext[0:leaves] = jnp.zeros((leaves, KR), f32)
+
+    @pl.when(jnp.logical_not(has_next))
+    def _():
+        xa[...] = jnp.zeros_like(xa)
+        coef_ext[2 * leaves : 3 * leaves] = jnp.zeros((leaves, KR), f32)
+
+    enough = nleaf + ngroup - 2
+    crossing = cross_next | cross_prev
+
+    @pl.when(crossing)
+    def _():
+        pl.semaphore_wait(barrier, enough + 1)
+
+    @pl.when(jnp.logical_not(crossing))
+    def _():
+        pl.semaphore_wait(barrier, enough)
+
+    def to_next(src, dst, sem):
+        return pltpu.make_async_remote_copy(
+            src_ref=src, dst_ref=dst, send_sem=sem.at[0], recv_sem=sem.at[2], device_id=next_id, device_id_type=MESH)
+
+    def to_prev(src, dst, sem):
+        return pltpu.make_async_remote_copy(
+            src_ref=src, dst_ref=dst, send_sem=sem.at[1], recv_sem=sem.at[3], device_id=prev_id, device_id_type=MESH)
+
+    moves = (
+        (x_hbm, xb, xa, x_sem),
+        (coef_ref, coef_ext.at[pl.ds(0, leaves)], coef_ext.at[pl.ds(2 * leaves, leaves)], coef_sem),
+    )
+
+    def send(move):
+        src, before, after, sem = move
+
+        @pl.when(has_next)
+        def _():
+            to_next(src, before, sem).start()
+
+        @pl.when(has_prev)
+        def _():
+            to_prev(src, after, sem).start()
+
+    send(moves[0])
+
+    def finish(move):
+        src, before, after, sem = move
+
+        @pl.when(has_next)
+        def _():
+            to_next(src, before, sem).wait_send()
+            to_prev(src, after, sem).wait_recv()
+
+        @pl.when(has_prev)
+        def _():
+            to_prev(src, after, sem).wait_send()
+            to_next(src, before, sem).wait_recv()
+
+    for c in range(K * LEAF // LANES):
+        basis_ref[:, c, :] = basis_in_ref[:, c * LANES : (c + 1) * LANES]
+    x_copy.wait()
+    coef_kernel(x_ref, basis_ref, coef_blocks)
+    ct[...] = jnp.zeros_like(ct)
+    for c in range(K // 2):
+        ct[c * 2 * RHS : (c + 1) * 2 * RHS, 0:leaves] = coef_blocks[:, c, :].T
+    for c in range(KR // LANES):
+        rows = slice(c * LANES, (c + 1) * LANES)
+        coef_ref[:, rows] = ct[rows, 0:LANES].T[:leaves]
+    coef_ext[leaves : 2 * leaves] = coef_ref[...]
+    send(moves[1])
+
     small_ref[...] = jnp.zeros_like(small_ref)
     small_ref[0:wide] = cluster_coupling_ref[...]
     small_ref[wide : wide + ngroup] = group_coupling_ref[...]
@@ -180,65 +253,6 @@
     turn(small_ref, 0, st, 0)
     transfer_copy.wait()
     turn(transfer_ref, 0, et, 0)
-    coef_ext[leaves : 2 * leaves] = coef_ref[...]
-
-    @pl.when(jnp.logical_not(has_prev))
-    def _():
-        xb[...] = jnp.zeros_like(xb)
-        coef_ext[0:leaves] = jnp.zeros((leaves, KR), f32)
-
-    @pl.when(jnp.logical_not(has_next))
-    def _():
-        xa[...] = jnp.zeros_like(xa)
-        coef_ext[2 * leaves : 3 * leaves] = jnp.zeros((leaves, KR), f32)
-
-    enough = nleaf + ngroup - 2
-    crossing = cross_next | cross_prev
-
-    @pl.when(crossing)
-    def _():
-        pl.semaphore_wait(barrier, enough + 1)
-
-    @pl.when(jnp.logical_not(crossing))
-    def _():
-        pl.semaphore_wait(barrier, enough)
-
-    def to_next(src, dst, sem):
-        return pltpu.make_async_remote_copy(
-            src_ref=src, dst_ref=dst, send_sem=sem.at[0], recv_sem=sem.at[2], device_id=next_id, device_id_type=MESH)
-
-    def to_prev(src, dst, sem):
-        return pltpu.make_async_remote_copy(
-            src_ref=src, dst_ref=dst, send_sem=sem.at[1], recv_sem=sem.at[3], device_id=prev_id, device_id_type=MESH)
-
-    moves = (
-        (x_hbm, xb, xa, x_sem),
-        (coef_ref, coef_ext.at[pl.ds(0, leaves)], coef_ext.at[pl.ds(2 * leaves, leaves)], coef_sem),
-    )
-
-    @pl.when(has_next)
-    def _():
-        for src, before, after, sem in moves:
-            to_next(src, before, sem).start()
-
-    @pl.when(has_prev)
-    def _():
-        for src, before, after, sem in moves:
-            to_prev(src, after, sem).start()
-
-    def finish(move):
-        src, before, after, sem = move
-
-        @pl.when(has_next)
-        def _():
-            to_next(src, before, sem).wait_send()
-            to_prev(src, after, sem).wait_recv()
-
-        @pl.when(has_prev)
-        def _():
-            to_prev(src, after, sem).wait_send()
-            to_next(src, before, sem).wait_recv()
-
     small_products(et, ct, work, 1)
     t, q = iota((LANES, LANES), 0), iota((LANES, LANES), 1)
     chosen = mask((q - base == t // per) & (t < leaves))
@@ -279,7 +293,6 @@
     lax.fori_loop(1, nleaf, start_leaf, 0)
     gathered_ref[z] = block_ref[...]
 
-    x_copy.wait()
     build(x_ref, 1)
     xh_ref[3 * leaves] = jnp.zeros(xh_ref.shape[1:], bf16)
     xl_ref[3 * leaves] = jnp.zeros(xl_ref.shape[1:], bf16)
@@ -389,9 +402,8 @@
     small_products(et, small_g, work, 1, transposed=True)
     gather = mask(iota((slots, LANES), 0) // FAR0 == iota((slots, LANES), 1))
     field = work[...] + pick(lwork[...], gather)
-    for c in range(KR // LANES):
-        rows_c = slice(c * LANES, (c + 1) * LANES)
-        field_ref[:, rows_c] = field[rows_c].T[:leaves]
+    for c in range(K // 2):
+        field_ref[:, c, :] = field[c * 2 * RHS : (c + 1) * 2 * RHS].T[:leaves]
 
 
 def sum_kernel(near_ref, basis_ref, field_ref, out_ref):
@@ -436,16 +448,6 @@
     leaves = near_blocks.shape[0]
     cpd = cluster_coupling.shape[0]
     ngroup, nleaf = lax.axis_size("group"), lax.axis_size("leaf")
-    basis3 = basis.reshape(leaves, K * LEAF // LANES, LANES)
-    coef = pl.pallas_call(
-        coef_kernel,
-        out_shape=jax.ShapeDtypeStruct((leaves, K // 2, 2 * RHS), f32),
-        in_specs=[VMEM, VMEM],
-        out_specs=VMEM,
-        compiler_params=params(),
-        name="leaf_coefficients",
-    )(right_sides, basis3)
-    coef = coef.reshape(leaves, KR)
     wide = cpd * FAR1
     base = wide + 8
     assert ngroup <= 8 and cpd <= 8 and base + 8 <= LANES and leaves <= LANES
@@ -453,15 +455,18 @@
     padded = -(-rows // LANES) * LANES
     source_lanes = -(-3 * leaves // LANES) * LANES
     slots = leaves * FAR0
-    near, field = pl.pallas_call(
+    near, field, basis3 = pl.pallas_call(
         functools.partial(tree_kernel, base, cpd, nleaf, ngroup),
         out_shape=(
             jax.ShapeDtypeStruct((RHS, leaves * LEAF), f32),
-            jax.ShapeDtypeStruct((leaves, KR), f32),
+            jax.ShapeDtypeStruct((leaves, K // 2, 2 * RHS), f32),
+            jax.ShapeDtypeStruct((leaves, K * LEAF // LANES, LANES), f32),
         ),
         in_specs=[SMEM] * 2 + [VMEM] * 6 + [pl.BlockSpec(memory_space=pl.ANY)] * 4,
-        out_specs=(VMEM, VMEM),
+        out_specs=(VMEM, VMEM, VMEM),
         scratch_shapes=[
+            pltpu.VMEM((leaves, K // 2, 2 * RHS), f32),
+            pltpu.VMEM((leaves, KR), f32),
             pltpu.VMEM((RHS, leaves * LEAF), f32),
             pltpu.VMEM((leaves, KK), f32),
             pltpu.VMEM((base + 8, KK), f32),
@@ -500,7 +505,7 @@
     )(
         near_source.T,
         near_count,
-        coef,
+        basis,
         leaf_source.T,
         cluster_source,
         cluster_coupling.reshape(wide, KK),
@@ -511,7 +516,6 @@
         near_blocks,
         leaf_coupling.reshape(slots, KK),
     )
-    field = field.reshape(leaves, K // 2, 2 * RHS)
     return pl.pallas_call(
         sum_kernel,
         out_shape=jax.ShapeDtypeStruct((RHS, leaves * LEAF), f32),

time: 44.8 us -> 41.7 us (0.931)
  local copies, waits for them, and re-layouts: 5.38 us -> 3.03 us
  Pallas kernels: 39.1 us -> 38.4 us
    pallas_call x1 -> x0, Pallas kernels: 1.29 us -> none  [per_device(): pl.pallas_call(coef_kernel, out_shape=jax.ShapeDtypeStruct((leaves, K //...]
    pallas_call x2 -> x0, local copies, waits for them, and re-layouts: 1.29 us -> none  [the longest x1 1.03 us: per_device(): pl.pallas_call(functools.partial(tree_kernel, base, cpd, nleaf, ngroup),...]
    reshape x2 -> x0, local copies, waits for them, and re-layouts: 1.06 us -> none  [the longest x1 0.78 us: per_device(): coef = coef.reshape(leaves, KR)]
    pallas_call x1, Pallas kernels: 35 us -> 35.6 us  [per_device(): pl.pallas_call(functools.partial(tree_kernel, base, cpd, nleaf, ngroup),...]
    unnamed x5 -> x6, local copies, waits for them, and re-layouts: 3.02 us -> 3.03 us
where the time goes in v4:
time: 41.7 us; the launch traced here: 41.4 us
  Pallas kernels  38.4 us (92%)
  local copies, waits for them, and re-layouts  3.03 us (7%)
    pallas_call x1, Pallas kernels, per_device(): pl.pallas_call(functools.partial(tree_kernel, base, cpd, nleaf, ngroup),...  35.6 us
    unnamed x6, local copies, waits for them, and re-layouts  3.03 us
    pallas_call x1, Pallas kernels, per_device(): pl.pallas_call(sum_kernel, out_shape=jax.ShapeDtypeStruct((RHS, leaves *...  2.84 us

profile of v4, /device:TPU:0, one launch (start us, length us, event | category | flops | bytes accessed | tf_op | source)
XLA Modules:
  0.0 41.4 jit_solution(3071774709618316648)
XLA Ops:
  0.0 35.6 %tree_and_near.1 = (f32[16,4096]{1,0:T(8,128)}, f32[64,16,32]{2,1,0:T(8,128)}, f32[64,16,128]{2,1,0:T(8,128)}) custom-call(s32[8,64]{1,0:T(8,128)} %bitcast.8, s32[64]{0:T(128)} %count_ref.1, f32[64,2048]{1,0:T(8,128)} %basis_in_ref.1, s32[8,64]{1,0:T(8,128)} %bitcast.9, s32[4,8]{1,0:T(4,128)} %cluster_source_ref.1, f32[32,1024]{1,0:T(8,128)} %bitcast.6, ...), custom_call_target="tpu_custom_call" | custom-call | tf_op jit(solution)/shard_map/tree_and_near/pallas_call | solution.py:458
  35.6 0.0 copy-start
  35.6 1.0 %copy-done = f32[64,16,32]{2,1,0:T(8,128)S(1)} copy-done((f32[64,16,32]{2,1,0:T(8,128)S(1)}, f32[64,16,32]{2,1,0:T(8,128)}, u32[]{:S(2)}) %copy-start) | copy-done | bytes 131096
  36.6 0.0 copy-start.1
  36.6 1.0 %copy-done.1 = f32[64,16,128]{2,1,0:T(8,128)S(1)} copy-done((f32[64,16,128]{2,1,0:T(8,128)S(1)}, f32[64,16,128]{2,1,0:T(8,128)}, u32[]{:S(2)}) %copy-start.1) | copy-done | bytes 524312
  37.7 0.0 copy-start.2
  37.7 0.9 %copy-done.2 = f32[16,4096]{1,0:T(8,128)S(1)} copy-done((f32[16,4096]{1,0:T(8,128)S(1)}, f32[16,4096]{1,0:T(8,128)}, u32[]{:S(2)}) %copy-start.2) | copy-done | bytes 262168
  38.6 2.8 %sum.1 = f32[16,4096]{1,0:T(8,128)} custom-call(f32[16,4096]{1,0:T(8,128)S(1)} %copy-done.2, f32[64,16,128]{2,1,0:T(8,128)S(1)} %copy-done.1, f32[64,16,32]{2,1,0:T(8,128)S(1)} %copy-done), custom_call_target="tpu_custom_call" | custom-call | tf_op jit(solution)/shard_map/sum/pallas_call | solution.py:519
Async XLA Ops:
  35.6 1.0 %copy-start = (f32[64,16,32]{2,1,0:T(8,128)S(1)}, f32[64,16,32]{2,1,0:T(8,128)}, u32[]{:S(2)}) copy-start(f32[64,16,32]{2,1,0:T(8,128)} %get-tuple-element.10.field_ref) | copy-start | bytes 393220
  36.6 1.0 %copy-start.1 = (f32[64,16,128]{2,1,0:T(8,128)S(1)}, f32[64,16,128]{2,1,0:T(8,128)}, u32[]{:S(2)}) copy-start(f32[64,16,128]{2,1,0:T(8,128)} %get-tuple-element.9.basis_ref) | copy-start | bytes 1572868
  37.7 0.9 %copy-start.2 = (f32[16,4096]{1,0:T(8,128)S(1)}, f32[16,4096]{1,0:T(8,128)}, u32[]{:S(2)}) copy-start(f32[16,4096]{1,0:T(8,128)} %get-tuple-element.8.near_ref) | copy-start | bytes 786436

commit v5 on v4

--- a/solution.py
+++ b/solution.py
@@ -112,8 +112,8 @@
                 source_ref, count_ref, basis_in_ref, leaf_source_ref, cluster_source_ref,
                 cluster_coupling_ref, group_coupling_ref, cluster_transfer_ref,
                 x_hbm, transfer_hbm, near_hbm, coupling_hbm,
-                near_out, field_ref, basis_ref,
-                coef_blocks, coef_ref, x_ref, transfer_ref, small_ref, near_ref, coupling_ref, xb, xa, coef_ext, block_ref, gathered_ref, group_ref, sums,
+                out_ref,
+                near_out, field_ref, basis_ref, coef_blocks, coef_ref, x_ref, transfer_ref, small_ref, near_ref, coupling_ref, xb, xa, coef_ext, block_ref, gathered_ref, group_ref, sums,
                 xh_ref, xl_ref, place_ref, part_ref,
                 et, ct, st, lt, gt, gl, work, lwork, small_g,
                 local_sem, x_sem, coef_sem, leaf_send, leaf_recv, group_send, group_recv):
@@ -404,6 +404,7 @@
     field = work[...] + pick(lwork[...], gather)
     for c in range(K // 2):
         field_ref[:, c, :] = field[c * 2 * RHS : (c + 1) * 2 * RHS].T[:leaves]
+    sum_kernel(near_out, basis_ref, field_ref, out_ref)
 
 
 def sum_kernel(near_ref, basis_ref, field_ref, out_ref):
@@ -455,16 +456,15 @@
     padded = -(-rows // LANES) * LANES
     source_lanes = -(-3 * leaves // LANES) * LANES
     slots = leaves * FAR0
-    near, field, basis3 = pl.pallas_call(
+    return pl.pallas_call(
         functools.partial(tree_kernel, base, cpd, nleaf, ngroup),
-        out_shape=(
-            jax.ShapeDtypeStruct((RHS, leaves * LEAF), f32),
-            jax.ShapeDtypeStruct((leaves, K // 2, 2 * RHS), f32),
-            jax.ShapeDtypeStruct((leaves, K * LEAF // LANES, LANES), f32),
-        ),
+        out_shape=jax.ShapeDtypeStruct((RHS, leaves * LEAF), f32),
         in_specs=[SMEM] * 2 + [VMEM] * 6 + [pl.BlockSpec(memory_space=pl.ANY)] * 4,
-        out_specs=(VMEM, VMEM, VMEM),
+        out_specs=VMEM,
         scratch_shapes=[
+            pltpu.VMEM((RHS, leaves * LEAF), f32),
+            pltpu.VMEM((leaves, K // 2, 2 * RHS), f32),
+            pltpu.VMEM((leaves, K * LEAF // LANES, LANES), f32),
             pltpu.VMEM((leaves, K // 2, 2 * RHS), f32),
             pltpu.VMEM((leaves, KR), f32),
             pltpu.VMEM((RHS, leaves * LEAF), f32),
@@ -516,14 +516,6 @@
         near_blocks,
         leaf_coupling.reshape(slots, KK),
     )
-    return pl.pallas_call(
-        sum_kernel,
-        out_shape=jax.ShapeDtypeStruct((RHS, leaves * LEAF), f32),
-        in_specs=[VMEM] * 3,
-        out_specs=VMEM,
-        compiler_params=params(),
-        name="sum",
-    )(near, basis3, field)
 
 
 def solution(mesh):

time: 41.7 us -> 39.3 us (0.942)
  local copies, waits for them, and re-layouts: 3.03 us -> 1.67 us
  Pallas kernels: 38.4 us -> 37.5 us
    pallas_call x1 -> x0, Pallas kernels: 2.84 us -> none  [per_device(): pl.pallas_call(sum_kernel, out_shape=jax.ShapeDtypeStruct((RHS, leaves *...]
    pallas_call x1, Pallas kernels: 35.6 us -> 37.5 us  [per_device(): pl.pallas_call(functools.partial(tree_kernel, base, cpd, nleaf, ngroup),...]
    unnamed x6 -> x1, local copies, waits for them, and re-layouts: 3.03 us -> 1.67 us
where the time goes in v5:
time: 39.3 us; the launch traced here: 39.1 us
  Pallas kernels  37.5 us (95%)
  local copies, waits for them, and re-layouts  1.67 us (4%)
    pallas_call x1, Pallas kernels, per_device(): pl.pallas_call(functools.partial(tree_kernel, base, cpd, nleaf, ngroup),...  37.5 us
    unnamed x1, local copies, waits for them, and re-layouts  1.67 us

profile of v5, /device:TPU:0, one launch (start us, length us, event | category | flops | bytes accessed | tf_op | source)
XLA Modules:
  0.0 39.1 jit_solution(12087037587080596887)
XLA Ops:
  0.0 37.5 %tree_and_near.1 = f32[16,4096]{1,0:T(8,128)} custom-call(s32[8,64]{1,0:T(8,128)} %bitcast.8, s32[64]{0:T(128)} %count_ref.1, f32[64,2048]{1,0:T(8,128)} %basis_in_ref.1, s32[8,64]{1,0:T(8,128)} %bitcast.9, s32[4,8]{1,0:T(4,128)} %cluster_source_ref.1, f32[32,1024]{1,0:T(8,128)} %bitcast.6, f32[4,1024]{1,0:T(4,128)} %bitcast.7, ...), custom_call_target="tpu_custom_call" | custom-call | tf_op jit(solution)/shard_map/tree_and_near/pallas_call | solution.py:459
  37.5 1.7 %copy.14 = f32[16,4096]{1,0:T(8,128)} copy(f32[16,4096]{1,0:T(8,128)} %tree_and_near.1) | data formatting | bytes 524288
